TPU v7x, 128 devices: a whole 4x4x4 slice. The times are simulated.
128 devices in a mesh: dp: 4 (over x), fsdp: 32 (over z, y, core).
Axes of the slice: x: 4, y: 4, z: 4, core: 2. Of those that a mesh axis runs over, the one named last changes fastest.
Arguments:
- features: bfloat16 [49152, 3072], P(('dp', 'fsdp')), may hold values from -20 to 20
- cotangent: bfloat16 [49152, 3072], P(('dp', 'fsdp')), may hold values from -6 to 6
- weight: bfloat16 [3072, 3072], P('fsdp'), may hold values from -0.109375 to 0.109375
Outputs:
- sharp_grad: float32 [3072, 3072], P('fsdp')
All inputs are finite; a program needn't handle non-finite values.
Results may differ from a plain program's by a relative error of at most 0.03.
Values may be sent and summed in bfloat16 or wider, within the bound.
A program may use at most 128 MiB of HBM per device.

v0:
```python
import jax
import jax.numpy as jnp
from jax import lax
from jax.sharding import PartitionSpec as P


def local_delta(features, cotangent):
    width = cotangent.shape[1]

    def fold_rows(total, piece, start):
        return jnp.dot(features, piece, preferred_element_type=jnp.float32)

    return (fold_rows, jnp.zeros((features.shape[0], width), jnp.float32))


def make_delta(act, cotangent, total_tokens):
    scaled = cotangent.astype(jnp.float32) / jnp.sqrt(jnp.float32(total_tokens))
    _, pull = jax.vjp(lambda v: jax.nn.gelu(v, approximate=True), act)
    return pull(scaled)[0].astype(jnp.bfloat16)


def body(features, cotangent, weight):
    width = weight.shape[1]
    total_tokens = features.shape[0] * lax.axis_size("dp") * lax.axis_size("fsdp")
    fold_rows, empty = local_delta(features, cotangent)
    act_first = fold_rows(empty, lax.all_gather(weight, "fsdp", axis=0, tiled=True), jnp.int32(0))
    delta_first = make_delta(act_first, cotangent, total_tokens)
    columns = features
    partial_first = lax.psum_scatter(
        jnp.einsum("tr,tc->rc", columns, delta_first, preferred_element_type=jnp.float32).astype(
            jnp.bfloat16
        ),
        "fsdp",
        scatter_dimension=0,
        tiled=True,
    )
    radius = 0.3 * jnp.sqrt(jnp.float32(width))
    first = lax.psum(partial_first, "dp").astype(jnp.float32)
    squares = lax.psum(jnp.sum(first * first), "fsdp")
    norm = jnp.sqrt(squares + 1e-06)
    perturbed = (weight.astype(jnp.float32) + radius * first / norm).astype(jnp.bfloat16)
    act_second = fold_rows(
        empty, lax.all_gather(perturbed, "fsdp", axis=0, tiled=True), jnp.int32(0)
    )
    delta_second = make_delta(act_second, cotangent, total_tokens)
    columns = features
    partial_second = lax.psum_scatter(
        jnp.einsum("tr,tc->rc", columns, delta_second, preferred_element_type=jnp.float32).astype(
            jnp.bfloat16
        ),
        "fsdp",
        scatter_dimension=0,
        tiled=True,
    )
    return lax.psum(partial_second, "dp").astype(jnp.float32)


def solution(mesh):
    in_specs = (P(("dp", "fsdp"), None), P(("dp", "fsdp"), None), P("fsdp", None))
    out_specs = P("fsdp", None)
    return jax.shard_map(body, mesh=mesh, in_specs=in_specs, out_specs=out_specs, check_vma=False)
```

profile of v0, /device:TPU:1, one launch (start us, length us, event | category | flops | bytes accessed | tf_op | source)
XLA Modules:
  0.0 673.7 jit_solution(16287378125968258587)
XLA Ops:
  6.5 0.0 copy-start
  6.5 0.0 all-gather.3.cloned.1.call-start
  6.5 0.7 all-gather.3.cloned.1.call-update
  7.3 0.0 reduce-scatter.7.cloned.1.call-start
  7.3 83.5 %all-gather.3.cloned.1.call-done = bf16[3072,3072]{1,0:T(8,128)(2,1)} async-done(((bf16[96,3072]{1,0:T(8,128)(2,1)}), bf16[3072,3072]{1,0:T(8,128)(2,1)}) %all-gather.3.cloned.1.call-update) | async-done | bytes 18874384 | tf_op jit(solution)/shard_map/all_gather | solution.py:26
  90.8 0.0 copy-done
  90.8 25.4 %convert_bitcast_fusion.1 = bf16[3072,3072]{0,1:T(8,128)(2,1)} fusion(bf16[384,3072]{1,0:T(8,128)(2,1)S(1)} %copy-done, bf16[384,3072]{1,0:T(8,128)(2,1)} %param.4, bf16[3072,3072]{1,0:T(8,128)(2,1)} %all-gather.3.cloned.1.call-done), kind=kOutput, calls=%fused_computation.1 | convolution fusion | flops 14530904064 | bytes 42467328 | tf_op jit(solution)/shard_map/tr,tc->rc/dot_general | solution.py:30
  116.2 24.7 %copy.15 = bf16[3072,3072]{1,0:T(8,128)(2,1)} copy(bf16[3072,3072]{0,1:T(8,128)(2,1)} %convert_bitcast_fusion.1) | data formatting | bytes 37748736
  140.8 0.0 copy-start.2
  140.8 0.0 reduce-scatter.7.cloned.1.call-update
  140.9 0.0 all-reduce.3.cloned.1.call-start
  140.9 119.8 %reduce-scatter.7.cloned.1.call-done = bf16[96,3072]{1,0:T(8,128)(2,1)} async-done(((bf16[3072,3072]{1,0:T(8,128)(2,1)}), bf16[96,3072]{1,0:T(8,128)(2,1)}) %reduce-scatter.7.cloned.1.call-update) | async-done | bytes 589840 | tf_op jit(solution)/shard_map/reduce_scatter | solution.py:29
  260.7 0.0 all-reduce.3.cloned.1.call-update
  260.7 0.0 all-gather.5.cloned.1.call-start
  260.7 44.0 %all-reduce.3.cloned.1.call-done = bf16[96,3072]{1,0:T(8,128)(2,1)} async-done(((bf16[96,3072]{1,0:T(8,128)(2,1)}), bf16[96,3072]{1,0:T(8,128)(2,1)}) %all-reduce.3.cloned.1.call-update) | async-done | bytes 589840 | tf_op jit(solution)/shard_map/psum | solution.py:38
  304.8 2.0 fusion.27
  306.8 65.3 %psum.22 = f32[]{:T(128)} all-reduce(f32[]{:T(128)} %fusion.27), channel_id=1, replica_groups=mesh['dp'=4,'fsdp'=32] {'fsdp'}, use_global_device_ids=true, to_apply=%region_3.0 | all-reduce | flops 1 | bytes 8 | tf_op jit(solution)/shard_map/psum | solution.py:39
  372.7 0.0 copy-done.2
  372.7 2.1 fusion.26
  374.8 0.0 all-gather.5.cloned.1.call-update
  374.9 0.2 reduce-scatter.9.cloned.1.call-start
  375.1 75.8 %all-gather.5.cloned.1.call-done = bf16[3072,3072]{1,0:T(8,128)(2,1)} async-done(((bf16[96,3072]{1,0:T(8,128)(2,1)}), bf16[3072,3072]{1,0:T(8,128)(2,1)}) %all-gather.5.cloned.1.call-update) | async-done | bytes 18874384 | tf_op jit(solution)/shard_map/all_gather | solution.py:43
  450.9 25.4 %convert_bitcast_fusion = bf16[3072,3072]{0,1:T(8,128)(2,1)} fusion(bf16[384,3072]{1,0:T(8,128)(2,1)S(1)} %copy-done, bf16[384,3072]{1,0:T(8,128)(2,1)} %param.4, bf16[3072,3072]{1,0:T(8,128)(2,1)} %all-gather.5.cloned.1.call-done), kind=kOutput, calls=%fused_computation | convolution fusion | flops 14530904064 | bytes 42467328 | tf_op jit(solution)/shard_map/tr,tc->rc/dot_general | solution.py:48
  476.3 24.7 %copy.17 = bf16[3072,3072]{1,0:T(8,128)(2,1)} copy(bf16[3072,3072]{0,1:T(8,128)(2,1)} %convert_bitcast_fusion) | data formatting | bytes 37748736
  501.0 0.0 reduce-scatter.9.cloned.1.call-update
  501.0 0.0 copy-start.1
  501.0 0.0 all-reduce.5.cloned.1.call-start
  501.0 119.8 %reduce-scatter.9.cloned.1.call-done = bf16[96,3072]{1,0:T(8,128)(2,1)} async-done(((bf16[3072,3072]{1,0:T(8,128)(2,1)}), bf16[96,3072]{1,0:T(8,128)(2,1)}) %reduce-scatter.9.cloned.1.call-update) | async-done | bytes 589840 | tf_op jit(solution)/shard_map/reduce_scatter | solution.py:47
  620.8 0.0 all-reduce.5.cloned.1.call-update
  620.8 43.8 %all-reduce.5.cloned.1.call-done = bf16[96,3072]{1,0:T(8,128)(2,1)} async-done(((bf16[96,3072]{1,0:T(8,128)(2,1)}), bf16[96,3072]{1,0:T(8,128)(2,1)}) %all-reduce.5.cloned.1.call-update) | async-done | bytes 589840 | tf_op jit(solution)/shard_map/psum | solution.py:55
  664.6 2.2 convert_element_type.44
  666.8 0.0 copy-done.1
Async XLA Ops:
  6.5 84.3 %copy-start = (bf16[384,3072]{1,0:T(8,128)(2,1)S(1)}, bf16[384,3072]{1,0:T(8,128)(2,1)}, u32[]{:S(2)}) copy-start(bf16[384,3072]{1,0:T(8,128)(2,1)} %param.3) | copy-start | bytes 7077892
  6.5 84.3 %all-gather.3.cloned.1.call-start = ((), (), s32[]{:S(2)}) async-start(), calls=%async_computation.2 | async-start | bytes 19464192 | tf_op jit(solution)/shard_map/all_gather | solution.py:26
  7.3 253.4 %reduce-scatter.7.cloned.1.call-start = ((), (), s32[]{:S(2)}) async-start(), calls=%async_computation.6 | async-start | bytes 19464192 | tf_op jit(solution)/shard_map/reduce_scatter | solution.py:29
  140.8 231.9 %copy-start.2 = (bf16[96,3072]{1,0:T(8,128)(2,1)S(1)}, bf16[96,3072]{1,0:T(8,128)(2,1)}, u32[]{:S(2)}) copy-start(bf16[96,3072]{1,0:T(8,128)(2,1)} %param.5) | copy-start | bytes 1769476
  140.9 163.9 %all-reduce.3.cloned.1.call-start = ((), (), s32[]{:S(2)}) async-start(), calls=%async_computation.3 | async-start | bytes 1179648 | tf_op jit(solution)/shard_map/psum | solution.py:38
  260.7 190.2 %all-gather.5.cloned.1.call-start = ((), (), s32[]{:S(2)}) async-start(), calls=%async_computation.4 | async-start | bytes 19464192 | tf_op jit(solution)/shard_map/all_gather | solution.py:43
  374.9 245.9 %reduce-scatter.9.cloned.1.call-start = ((), (), s32[]{:S(2)}) async-start(), calls=%async_computation.7 | async-start | bytes 19464192 | tf_op jit(solution)/shard_map/reduce_scatter | solution.py:47
  501.0 165.8 %copy-start.1 = (bf16[384,3072]{1,0:T(8,128)(2,1)S(1)}, bf16[384,3072]{1,0:T(8,128)(2,1)}, u32[]{:S(2)}) copy-start(bf16[384,3072]{1,0:T(8,128)(2,1)} %param.3) | copy-start | bytes 7077892
  501.0 163.6 %all-reduce.5.cloned.1.call-start = ((), (), s32[]{:S(2)}) async-start(), calls=%async_computation.5 | async-start | bytes 1179648 | tf_op jit(solution)/shard_map/psum | solution.py:55
Sparse Core Ops, SparseCore 0:
  9.6 81.1 all-gather.2
  141.0 119.6 reduce-scatter.6
  263.1 41.6 all-reduce.2
  375.0 75.8 all-gather.4
  501.1 119.6 reduce-scatter.8
  623.0 41.5 all-reduce.4
where the time goes:
time: 676 us; the launch traced here: 674 us
  waiting for transfers between devices  488 us (72%)
  blocking collectives  65.3 us (10%)
  matrix products  50.7 us (8%)
  local copies, waits for them, and re-layouts  49.3 us (7%)
  between operations  14.2 us (2%)
    reduce_scatter x1, waiting for transfers between devices, body(): lax.psum_scatter(jnp.einsum('tr,tc->rc', columns, delta_first, preferred_...  120 us
    reduce_scatter x1, waiting for transfers between devices, body(): lax.psum_scatter(jnp.einsum('tr,tc->rc', columns, delta_second, preferred...  120 us
    all_gather x1, waiting for transfers between devices, body(): lax.all_gather(weight, 'fsdp', axis=0, tiled=True)  83.5 us
    all_gather x1, waiting for transfers between devices, body(): lax.all_gather(perturbed, 'fsdp', axis=0, tiled=True)  75.8 us
    psum x1, blocking collectives, body(): squares = lax.psum(jnp.sum(first * first), 'fsdp')  65.3 us
    unnamed x8, local copies, waits for them, and re-layouts  49.3 us
    psum x1, waiting for transfers between devices, body(): first = lax.psum(partial_first, 'dp').astype(jnp.float32)  44 us
    psum x1, waiting for transfers between devices, body(): return lax.psum(partial_second, 'dp').astype(jnp.float32)  43.8 us
  transfers between devices with their start and end apart: 6, of which 6 were waited for; matrix products, arithmetic and copies ran while one was open for 0% of the time, Pallas kernels for 0%

commit v1 on v0

v1 whole, which is shorter than its diff:
```python
import jax
import jax.numpy as jnp
from jax import lax
from jax.sharding import PartitionSpec as P


def make_delta(act, cotangent, total_tokens):
    scaled = cotangent.astype(jnp.float32) / jnp.sqrt(jnp.float32(total_tokens))
    _, pull = jax.vjp(lambda v: jax.nn.gelu(v, approximate=True), act)
    return pull(scaled)[0].astype(jnp.bfloat16)


def body(features, cotangent, weight):
    width = weight.shape[1]
    groups = lax.axis_size("dp")
    total_tokens = features.shape[0] * groups * lax.axis_size("fsdp")
    share = width // groups
    radius = 0.3 * jnp.sqrt(jnp.float32(width))

    mine = lax.dynamic_slice_in_dim(weight, lax.axis_index("dp") * share, share, 1)
    full = lax.all_gather(mine, "fsdp", axis=0, tiled=True)
    cot = lax.all_to_all(cotangent, "dp", split_axis=1, concat_axis=0, tiled=True)
    feats = lax.all_gather(features, "dp", axis=0, tiled=True)

    def grad(v):
        act = jnp.dot(feats, v, preferred_element_type=jnp.float32)
        delta = make_delta(act, cot, total_tokens)
        term = jnp.einsum("tr,tc->rc", feats, delta, preferred_element_type=jnp.float32)
        return lax.psum_scatter(
            term.astype(jnp.bfloat16), "fsdp", scatter_dimension=0, tiled=True
        )

    first = grad(full).astype(jnp.float32)
    squares = lax.psum(jnp.sum(first * first), ("dp", "fsdp"))
    norm = jnp.sqrt(squares + 1e-06)
    perturbed = (mine.astype(jnp.float32) + radius * first / norm).astype(jnp.bfloat16)
    second = grad(lax.all_gather(perturbed, "fsdp", axis=0, tiled=True))
    return lax.all_gather(second, "dp", axis=1, tiled=True).astype(jnp.float32)


def solution(mesh):
    in_specs = (P(("dp", "fsdp"), None), P(("dp", "fsdp"), None), P("fsdp", None))
    out_specs = P("fsdp", None)
    return jax.shard_map(body, mesh=mesh, in_specs=in_specs, out_specs=out_specs, check_vma=False)
```

time: 676 us -> 523 us (0.77)
  waiting for transfers between devices: 488 us -> 313 us
  blocking collectives: 65.3 us -> 109 us
  local copies, waits for them, and re-layouts: 49.3 us -> 20.8 us
    psum x2 -> x0, waiting for transfers between devices: 87.9 us -> none  [the longest x1 44 us: body(): first = lax.psum(partial_first, 'dp').astype(jnp.float32)]
    reduce_scatter x2, waiting for transfers between devices: 240 us -> 164 us  [grad(): lax.psum_scatter(term.astype(jnp.bfloat16), 'fsdp', scatter_dimension=0,...]
    unnamed x8 -> x3, local copies, waits for them, and re-layouts: 49.3 us -> 16.3 us
    all_to_all x0 -> x1, blocking collectives: none -> 32.9 us  [body(): lax.all_to_all(cotangent, 'dp', split_axis=1, concat_axis=0, tiled=True)]
    all_gather x2 -> x3, waiting for transfers between devices: 159 us -> 148 us  [the longest x1 92.5 us: body(): feats = lax.all_gather(features, 'dp', axis=0, tiled=True)]
    all_gather x0 -> x1, blocking collectives: none -> 10.7 us  [body(): return lax.all_gather(second, 'dp', axis=1, tiled=True).astype(jnp.float32)]
  transfers between devices with their start and end apart: 6 -> 5, of which waited for: 6 -> 5; matrix products, arithmetic and copies ran while one was open for 0% -> 1% of each run, Pallas kernels for 0% -> 0%
where the time goes in v1:
time: 523 us; the launch traced here: 518 us
  waiting for transfers between devices  313 us (60%)
  blocking collectives  109 us (21%)
  matrix products  55.7 us (11%)
  local copies, waits for them, and re-layouts  20.8 us (4%)
  between operations  13.8 us (3%)
    reduce_scatter x2, waiting for transfers between devices, grad(): lax.psum_scatter(term.astype(jnp.bfloat16), 'fsdp', scatter_dimension=0,...  164 us
    all_gather x1, waiting for transfers between devices, body(): feats = lax.all_gather(features, 'dp', axis=0, tiled=True)  92.5 us
    psum x1, blocking collectives, body(): squares = lax.psum(jnp.sum(first * first), ('dp', 'fsdp'))  65.9 us
    dot_general x2, matrix products, grad(): jnp.einsum('tr,tc->rc', feats, delta, preferred_element_type=jnp.float32)  55.7 us
    all_gather x1, waiting for transfers between devices, body(): second = grad(lax.all_gather(perturbed, 'fsdp', axis=0, tiled=True))  43.7 us
    all_to_all x1, blocking collectives, body(): lax.all_to_all(cotangent, 'dp', split_axis=1, concat_axis=0, tiled=True)  32.9 us
    unnamed x3, local copies, waits for them, and re-layouts  16.3 us
    all_gather x1, waiting for transfers between devices, body(): full = lax.all_gather(mine, 'fsdp', axis=0, tiled=True)  12.1 us
  transfers between devices with their start and end apart: 5, of which 5 were waited for; matrix products, arithmetic and copies ran while one was open for 1% of the time, Pallas kernels for 0%

profile of v1, /device:TPU:1, one launch (start us, length us, event | category | flops | bytes accessed | tf_op | source)
XLA Modules:
  0.0 518.3 jit_solution(14874943143046056578)
XLA Ops:
  6.5 0.0 all-gather.4.cloned.1.call-start
  6.5 1.6 constant_dynamic-slice_fusion
  8.1 0.0 all-gather.4.cloned.1.call-update
  8.1 0.0 all-gather.6.cloned.1.call-start
  8.2 0.7 all-gather.6.cloned.1.call-update
  8.9 0.0 reduce-scatter.7.cloned.1.call-start
  8.9 3.0 copy.11
  11.9 32.9 %all_to_all.13 = bf16[384,4,768]{0,2,1:T(8,128)(2,1)S(1)} all-to-all(bf16[384,4,768]{0,2,1:T(8,128)(2,1)S(1)} %bitcast.49), channel_id=1, replica_groups=mesh['dp'=4,'fsdp'=32] {'dp'}, dimensions={1} | all-to-all | bytes 4718592 | tf_op jit(solution)/shard_map/all_to_all | solution.py:22
  44.8 0.4 multiply_bitcast_fusion
  45.2 2.9 copy.19
  48.2 12.1 %all-gather.4.cloned.1.call-done = bf16[3072,768]{1,0:T(8,128)(2,1)} async-done(((bf16[96,768]{1,0:T(8,128)(2,1)}), bf16[3072,768]{1,0:T(8,128)(2,1)}) %all-gather.4.cloned.1.call-update) | async-done | bytes 4718608 | tf_op jit(solution)/shard_map/all_gather | solution.py:21
  60.3 92.5 %all-gather.6.cloned.1.call-done = bf16[1536,3072]{1,0:T(8,128)(2,1)} async-done(((bf16[384,3072]{1,0:T(8,128)(2,1)}), bf16[1536,3072]{1,0:T(8,128)(2,1)}) %all-gather.6.cloned.1.call-update) | async-done | bytes 9437200 | tf_op jit(solution)/shard_map/all_gather | solution.py:23
  152.8 27.8 %fusion.18 = bf16[3072,768]{0,1:T(8,128)(2,1)} fusion(bf16[1536,3072]{1,0:T(8,128)(2,1)} %all-gather.6.cloned.1.call-done, f32[1536,768]{0,1:T(8,128)} %bitcast.50, bf16[3072,768]{1,0:T(8,128)(2,1)} %all-gather.4.cloned.1.call-done), kind=kOutput, calls=%fused_computation.27 | convolution fusion | flops 14521466880 | bytes 23592960 | tf_op jit(solution)/shard_map/tr,tc->rc/dot_general | solution.py:28
  180.6 6.7 %copy.15 = bf16[3072,768]{1,0:T(8,128)(2,1)} copy(bf16[3072,768]{0,1:T(8,128)(2,1)} %fusion.18) | data formatting | bytes 9437184
  187.3 0.0 reduce-scatter.7.cloned.1.call-update
  187.3 0.0 all-gather.8.cloned.1.call-start
  187.3 83.2 %reduce-scatter.7.cloned.1.call-done = bf16[96,768]{1,0:T(8,128)(2,1)} async-done(((bf16[3072,768]{1,0:T(8,128)(2,1)}), bf16[96,768]{1,0:T(8,128)(2,1)}) %reduce-scatter.7.cloned.1.call-update) | async-done | bytes 147472 | tf_op jit(solution)/shard_map/reduce_scatter | solution.py:29
  270.5 1.6 fusion.35
  272.1 65.9 %psum.7 = f32[]{:T(128)} all-reduce(f32[]{:T(128)} %fusion.35), channel_id=1, replica_groups=mesh['dp'=4,'fsdp'=32] {'dp','fsdp'}, use_global_device_ids=true, to_apply=%region_2.0 | all-reduce | flops 1 | bytes 8 | tf_op jit(solution)/shard_map/psum | solution.py:34
  338.7 1.7 fusion.34
  340.4 0.0 all-gather.8.cloned.1.call-update
  340.4 0.2 reduce-scatter.9.cloned.1.call-start
  340.7 43.7 %all-gather.8.cloned.1.call-done = bf16[3072,768]{1,0:T(8,128)(2,1)} async-done(((bf16[96,768]{1,0:T(8,128)(2,1)}), bf16[3072,768]{1,0:T(8,128)(2,1)}) %all-gather.8.cloned.1.call-update) | async-done | bytes 4718608 | tf_op jit(solution)/shard_map/all_gather | solution.py:37
  384.4 27.8 %fusion.19 = bf16[3072,768]{0,1:T(8,128)(2,1)} fusion(bf16[1536,3072]{1,0:T(8,128)(2,1)} %all-gather.6.cloned.1.call-done, f32[1536,768]{0,1:T(8,128)} %bitcast.51, bf16[3072,768]{1,0:T(8,128)(2,1)} %all-gather.8.cloned.1.call-done), kind=kOutput, calls=%fused_computation.28 | convolution fusion | flops 14521466880 | bytes 23592960 | tf_op jit(solution)/shard_map/tr,tc->rc/dot_general | solution.py:28
  412.2 6.6 %copy.17 = bf16[3072,768]{1,0:T(8,128)(2,1)} copy(bf16[3072,768]{0,1:T(8,128)(2,1)} %fusion.19) | data formatting | bytes 9437184
  418.9 0.0 reduce-scatter.9.cloned.1.call-update
  418.9 81.1 %reduce-scatter.9.cloned.1.call-done = bf16[96,768]{1,0:T(8,128)(2,1)} async-done(((bf16[3072,768]{1,0:T(8,128)(2,1)}), bf16[96,768]{1,0:T(8,128)(2,1)}) %reduce-scatter.9.cloned.1.call-update) | async-done | bytes 147472 | tf_op jit(solution)/shard_map/reduce_scatter | solution.py:29
  500.0 10.7 %all_gather.15 = bf16[96,3072]{1,0:T(8,128)(2,1)S(1)} all-gather(bf16[96,768]{1,0:T(8,128)(2,1)} %reduce-scatter.9.cloned.1.call-done), channel_id=1, replica_groups=mesh['dp'=4,'fsdp'=32] {'dp'}, dimensions={1}, use_global_device_ids=true | all-gather | bytes 737280 | tf_op jit(solution)/shard_map/all_gather | solution.py:38
  510.7 1.1 convert_element_type.46
Async XLA Ops:
  6.5 53.7 %all-gather.4.cloned.1.call-start = ((), (), s32[]{:S(2)}) async-start(), calls=%async_computation.3 | async-start | bytes 4866048 | tf_op jit(solution)/shard_map/all_gather | solution.py:21
  8.1 144.6 %all-gather.6.cloned.1.call-start = ((), (), s32[]{:S(2)}) async-start(), calls=%async_computation.4 | async-start | bytes 11796480 | tf_op jit(solution)/shard_map/all_gather | solution.py:23
  8.9 261.6 %reduce-scatter.7.cloned.1.call-start = ((), (), s32[]{:S(2)}) async-start(), calls=%async_computation.6 | async-start | bytes 4866048 | tf_op jit(solution)/shard_map/reduce_scatter | solution.py:29
  187.3 197.1 %all-gather.8.cloned.1.call-start = ((), (), s32[]{:S(2)}) async-start(), calls=%async_computation.5 | async-start | bytes 4866048 | tf_op jit(solution)/shard_map/all_gather | solution.py:37
  340.4 159.5 %reduce-scatter.9.cloned.1.call-start = ((), (), s32[]{:S(2)}) async-start(), calls=%async_computation.7 | async-start | bytes 4866048 | tf_op jit(solution)/shard_map/reduce_scatter | solution.py:29
Sparse Core Ops, SparseCore 0:
  9.6 50.6 all-gather.3
  61.9 90.7 all-gather.5
  187.4 83.0 reduce-scatter.6
  340.6 43.7 all-gather.7
  419.0 80.9 reduce-scatter.8

commit v2 on v1

v2 whole, which is shorter than its diff:
```python
import jax
import jax.numpy as jnp
from jax import lax
from jax.experimental import pallas as pl
from jax.experimental.pallas import tpu as pltpu
from jax.sharding import PartitionSpec as P

MESH = pl.DeviceIdType.MESH
F32 = jnp.float32
BF16 = jnp.bfloat16

RING = 4
TOK = 384
DI = 3072
DO = 3072
ROWS = 96
BLK = 256
NB = 3
SHARE = BLK * NB
PART = 128
PARTS = TOK // PART
N_SEMS = 256
ROOT = 0.7978845608028654
CUBIC = 0.044715


def kernel(
    feat, cot, weight, out,
    f, ft, c, d, v1, v2, a1, a2, g, r1, r2, t, tx, o, nown, nrecv, kvec,
    send_sems, recv_sems, local_sems,
):
    x = lax.axis_index("dp")
    ff = lax.axis_index("fsdp")
    z = ff // 8
    y = lax.rem(ff // 2, RING)
    core = lax.rem(ff, 2)
    s = 1 - 2 * core

    def wrap(v):
        return lax.rem(v + 2 * RING, RING)

    def dev(dx=0, dy=0, dz=0, other=False):
        cc = 1 - core if other else core
        return (wrap(x + dx), (wrap(z + dz) * RING + wrap(y + dy)) * 2 + cc)

    def ring_dev(axis, step):
        return dev(dy=step) if axis == "y" else dev(dz=step)

    counter = [0]
    pending = []

    def remote(src, dst, device):
        i = counter[0]
        counter[0] += 1
        cp = pltpu.make_async_remote_copy(
            src_ref=src, dst_ref=dst, send_sem=send_sems.at[i], recv_sem=recv_sems.at[i],
            device_id=device, device_id_type=MESH,
        )
        cp.start()
        pending.append(cp)
        return cp

    def drain():
        while pending:
            pending.pop().wait_send()

    local_counter = [0]

    def local(src, dst):
        i = local_counter[0]
        local_counter[0] += 1
        cp = pltpu.make_async_copy(src, dst, local_sems.at[i])
        cp.start()
        return cp

    def columns(dx, other, j):
        cc = 1 - core if other else core
        start = (lax.rem(x + dx + RING, 2) * 2 + cc) * SHARE + j * BLK
        return pl.ds(pl.multiple_of(start, BLK), BLK)

    w_own = [local(weight.at[:, columns(0, False, j)], v1.at[j, z, y, core]) for j in range(NB)]
    f_own = local(feat, f.at[0])
    c_own = [local(cot.at[:, columns(0, False, j)], c.at[j, 0]) for j in range(NB)]

    barrier = pltpu.get_barrier_semaphore()
    others = [dev(other=True)]
    for step in (1, 2, 3):
        others += [dev(dx=step), dev(dx=step, other=True), dev(dy=step), dev(dz=step)]
    for other in others:
        pl.semaphore_signal(barrier, inc=1, device_id=other, device_id_type=MESH)
    pl.semaphore_wait(barrier, len(others))

    sib = dev(other=True)
    w_sib = [
        remote(weight.at[:, columns(0, True, j)], v1.at[j, z, y, core], sib) for j in range(NB)
    ]
    f_x = []
    for k in range(PARTS):
        rows = pl.ds(k * PART, PART)
        f_x.append(remote(feat.at[rows], f.at[2, rows], dev(dx=s)))
    f_sib = remote(feat, f.at[1], sib)
    c_sib, c_x, c_xo = [], [], []
    for j in range(NB):
        c_sib.append(remote(cot.at[:, columns(0, True, j)], c.at[j, 1], sib))
    for j in range(NB):
        c_x.append(remote(cot.at[:, columns(1, False, j)], c.at[j, 2], dev(dx=s)))
        c_xo.append(remote(cot.at[:, columns(1, True, j)], c.at[j, 3], dev(dx=s, other=True)))

    class Gather:
        def __init__(self, v, j):
            self.v, self.j = v, j

        def piece(self, half, stage, step):
            axis = self.axis(half, stage)
            zz = wrap(z + step) if axis == "z" else z
            yy = wrap(y + step) if axis == "y" else y
            if stage == 1:
                return self.v.at[self.j, zz, yy, half]
            if axis == "z":
                return self.v.at[self.j, zz, :, half]
            return self.v.at[self.j, :, yy, half]

        def axis(self, half, stage):
            return ("y", "z")[(half + stage + 1) % 2]

        def start(self, stage):
            self.near, self.far, self.relay = {}, {}, {}
            for half in (0, 1):
                axis, own = self.axis(half, stage), self.piece(half, stage, 0)
                self.near[half] = remote(own, own, ring_dev(axis, s))
                self.far[half] = remote(own, own, ring_dev(axis, -s))

        def forward(self, stage):
            for half in (0, 1):
                self.near[half].wait_recv()
                got = self.piece(half, stage, -s)
                self.relay[half] = remote(got, got, ring_dev(self.axis(half, stage), s))

        def finish(self, stage):
            for half in (0, 1):
                self.far[half].wait_recv()
                self.relay[half].wait_recv()

    class Scatter:
        def __init__(self, j):
            self.j = j

        def axis(self, half, stage):
            return ("z", "y")[(half + stage + 1) % 2]

        def place(self, half, stage, step):
            axis = self.axis(half, stage)
            zz = wrap(z + step) if axis == "z" else z
            yy = wrap(y + step) if axis == "y" else y
            if stage == 2:
                return (self.j, zz, yy, half)
            if axis == "z":
                return (self.j, zz, slice(None), half)
            return (self.j, slice(None), yy, half)

        def land(self, half, stage, i):
            return (r1 if stage == 1 else r2).at[self.j, half, i]

        def start(self, stage):
            self.first, self.back, self.merged = {}, {}, {}
            for half in (0, 1):
                axis = self.axis(half, stage)
                self.first[half] = remote(
                    g.at[self.place(half, stage, 2)], self.land(half, stage, 0), ring_dev(axis, s)
                )
                self.back[half] = remote(
                    g.at[self.place(half, stage, -s)], self.land(half, stage, 1), ring_dev(axis, -s)
                )

        def middle(self, stage):
            for half in (0, 1):
                self.first[half].wait_recv()
                at = self.place(half, stage, s)
                if stage == 1:
                    got = r1[self.j, half, 0]
                else:
                    got = r2[self.j, half, 0]
                g[at] = (g[at].astype(F32) + got.astype(F32)).astype(BF16)
                self.merged[half] = remote(
                    g.at[at], self.land(half, stage, 2), ring_dev(self.axis(half, stage), s)
                )

        def finish(self, stage):
            for half in (0, 1):
                self.back[half].wait_recv()
                self.merged[half].wait_recv()
                at = self.place(half, stage, 0)
                r = r1 if stage == 1 else r2
                total = g[at].astype(F32) + r[self.j, half, 1].astype(F32) + r[self.j, half, 2].astype(F32)
                if stage == 1:
                    g[at] = total.astype(BF16)
                else:
                    t[self.j, half] = total.astype(BF16)

    def transpose(slot, part):
        @pl.loop(0, DI // BLK)
        def _(i):
            cols = pl.ds(pl.multiple_of(i * BLK, BLK), BLK)
            ft[cols, pl.ds(slot * TOK + part * PART, PART)] = f[slot, pl.ds(part * PART, PART), cols].T

    def matmul(j, v, dst, slots):
        lo, hi = slots

        @pl.loop(lo, hi)
        def _(slot):
            dst[slot] = jnp.dot(f[slot], v[j].reshape(DI, BLK), preferred_element_type=F32)

    def act(j, slots):
        matmul(j, v1, a1.at[j], slots)

    def delta(j, slots, second):
        lo, hi = slots
        step = 64

        @pl.loop(lo * (TOK // step), hi * (TOK // step))
        def _(i):
            slot = i // (TOK // step)
            rows = pl.ds(pl.multiple_of(lax.rem(i, TOK // step) * step, step), step)
            a = a1[j, slot, rows, :]
            if second:
                a = a + a2[slot, rows, :] * kvec[0:1, :]
            square = a * a
            th = jnp.tanh(ROOT * a * (1.0 + CUBIC * square))
            slope = 0.5 * (1.0 + th) + 0.5 * a * (1.0 - th * th) * (ROOT * (1.0 + 3.0 * CUBIC * square))
            scaled = c[j, slot, rows, :].astype(F32) * (1.0 / jnp.sqrt(F32(TOK * 128)))
            d[j, slot, rows, :] = (scaled * slope).astype(BF16)

    def grad(j):
        rows = DI // RING

        @pl.loop(0, RING)
        def _(i):
            left = ft[pl.ds(pl.multiple_of(i * rows, rows), rows), :]
            term = jnp.dot(left, d[j].reshape(4 * TOK, BLK), preferred_element_type=F32)
            g[j, i] = term.astype(BF16).reshape(RING, 2, ROWS, BLK)

    ag = [Gather(v1, j) for j in range(NB)]
    for j in range(NB):
        w_own[j].wait()
        w_sib[j].wait_recv()
        ag[j].start(1)
    f_own.wait()
    for k in range(PARTS):
        transpose(0, k)
    for j in range(NB):
        ag[j].forward(1)
    for j in range(NB):
        ag[j].finish(1)
        ag[j].start(2)
    f_sib.wait_recv()
    for k in range(PARTS):
        transpose(1, k)

    f_fwd = []

    def take_part(k):
        rows = pl.ds(k * PART, PART)
        f_x[k].wait_recv()
        f_fwd.append(remote(f.at[2, rows], f.at[3, rows], sib))
        transpose(2, k)

    def take_forwarded(k):
        f_fwd[k].wait_recv()
        transpose(3, k)

    for cp in c_own:
        cp.wait()
    for cp in c_sib:
        cp.wait_recv()
    ag[0].forward(2)
    take_part(0)
    ag[0].finish(2)
    act(0, (0, 2))
    delta(0, (0, 2), False)
    ag[1].forward(2)
    take_forwarded(0)
    take_part(1)
    ag[1].finish(2)
    act(1, (0, 2))
    delta(1, (0, 2), False)
    ag[2].forward(2)
    take_forwarded(1)
    ag[2].finish(2)
    act(2, (0, 2))
    delta(2, (0, 2), False)
    take_part(2)
    take_forwarded(2)

    def rest(j):
        act(j, (2, 4))
        c_x[j].wait_recv()
        c_xo[j].wait_recv()
        delta(j, (2, 4), False)
        grad(j)

    rs = [Scatter(j) for j in range(NB)]
    rest(0)
    rs[0].start(1)
    rest(1)
    rs[0].middle(1)
    rs[1].start(1)
    rest(2)
    rs[0].finish(1)
    rs[0].start(2)
    rs[1].middle(1)
    rs[2].start(1)

    swap = {}

    def cross(j):
        rs[j].finish(2)
        swap[j] = remote(t.at[j], tx.at[j], dev(dx=2))

    def first(j, squares):
        swap[j].wait_recv()
        total = t[j].astype(F32) + tx[j].astype(F32)
        v2[j, z, y] = total.astype(BF16)
        sq = (total * total).reshape(2 * ROWS // 8, 8, BLK).sum(axis=0)
        return squares + sq[:, :128] + sq[:, 128:]

    ag = [Gather(v2, j) for j in range(NB)]
    squares = jnp.zeros((8, 128), F32)
    rs[0].middle(2)
    rs[1].finish(1)
    rs[1].start(2)
    rs[2].middle(1)
    cross(0)
    rs[1].middle(2)
    rs[2].finish(1)
    rs[2].start(2)
    squares = first(0, squares)
    ag[0].start(1)
    cross(1)
    rs[2].middle(2)
    ag[0].forward(1)
    squares = first(1, squares)
    ag[1].start(1)
    cross(2)
    ag[0].finish(1)
    ag[0].start(2)
    ag[1].forward(1)
    squares = first(2, squares)
    ag[2].start(1)

    def norm_send(i, value, devices):
        nown[i] = value
        return [remote(nown.at[i], nrecv.at[i, n], device) for n, device in enumerate(devices)]

    def norm_add(i, copies):
        total = nown[i]
        for n, cp in enumerate(copies):
            cp.wait_recv()
            total = total + nrecv[i, n]
        return total

    ns = norm_send(0, squares, [sib, dev(dx=1), dev(dx=1, other=True)])
    ag[1].finish(1)
    ag[1].start(2)
    ag[2].forward(1)
    ns = norm_send(1, norm_add(0, ns), [dev(dy=n) for n in (1, 2, 3)])
    ag[0].forward(2)
    ag[2].finish(1)
    ag[2].start(2)
    ns = norm_send(2, norm_add(1, ns), [dev(dz=n) for n in (1, 2, 3)])
    ag[0].finish(2)
    matmul(0, v2, a2, (0, 4))
    ag[1].forward(2)
    total = jnp.sum(norm_add(2, ns), keepdims=True)
    factor = 0.3 * jnp.sqrt(F32(DO)) / jnp.sqrt(total + 1e-06)
    kvec[...] = jnp.broadcast_to(factor, kvec.shape)

    drain()
    rs = [Scatter(j) for j in range(NB)]
    delta(0, (0, 4), True)
    grad(0)
    rs[0].start(1)
    ag[1].finish(2)
    matmul(1, v2, a2, (0, 4))
    ag[2].forward(2)
    delta(1, (0, 4), True)
    rs[0].middle(1)
    grad(1)
    rs[1].start(1)
    ag[2].finish(2)
    matmul(2, v2, a2, (0, 4))
    rs[0].finish(1)
    rs[0].start(2)
    rs[1].middle(1)
    delta(2, (0, 4), True)
    grad(2)
    rs[2].start(1)
    rs[0].middle(2)
    rs[1].finish(1)
    rs[1].start(2)
    rs[2].middle(1)

    share = {}

    def spread(j):
        rs[j].finish(2)
        share[j] = [remote(t.at[j, 1 - core], o.at[j, 0, 1], sib)]
        for step in (1, 2, 3):
            share[j].append(remote(t.at[j, core], o.at[j, step, 0], dev(dx=step)))
            share[j].append(remote(t.at[j, 1 - core], o.at[j, step, 1], dev(dx=step, other=True)))

    def collect(j):
        for cp in share[j]:
            cp.wait_recv()
        for other in (False, True):
            same = t[j, core] if not other else o[j, 0, 1]
            k = int(other)
            out[:, columns(0, other, j)] = same.astype(F32) + o[j, 2, k].astype(F32)
            out[:, columns(1, other, j)] = o[j, 1, k].astype(F32) + o[j, 3, k].astype(F32)

    spread(0)
    rs[1].middle(2)
    rs[2].finish(1)
    rs[2].start(2)
    spread(1)
    rs[2].middle(2)
    collect(0)
    spread(2)
    collect(1)
    collect(2)
    drain()


def body(features, cotangent, weight):
    return pl.pallas_call(
        kernel,
        out_shape=jax.ShapeDtypeStruct((ROWS, DO), F32),
        in_specs=[pl.BlockSpec(memory_space=pl.ANY)] * 3,
        out_specs=pl.BlockSpec(memory_space=pltpu.VMEM),
        scratch_shapes=[
            pltpu.VMEM((4, TOK, DI), BF16),
            pltpu.VMEM((DI, 4 * TOK), BF16),
            pltpu.VMEM((NB, 4, TOK, BLK), BF16),
            pltpu.VMEM((NB, 4, TOK, BLK), BF16),
            pltpu.VMEM((NB, RING, RING, 2, ROWS, BLK), BF16),
            pltpu.VMEM((NB, RING, RING, 2, ROWS, BLK), BF16),
            pltpu.VMEM((NB, 4, TOK, BLK), F32),
            pltpu.VMEM((4, TOK, BLK), F32),
            pltpu.VMEM((NB, RING, RING, 2, ROWS, BLK), BF16),
            pltpu.VMEM((NB, 2, 3, RING, ROWS, BLK), BF16),
            pltpu.VMEM((NB, 2, 3, ROWS, BLK), BF16),
            pltpu.VMEM((NB, 2, ROWS, BLK), BF16),
            pltpu.VMEM((NB, 2, ROWS, BLK), BF16),
            pltpu.VMEM((NB, 4, 2, ROWS, BLK), BF16),
            pltpu.VMEM((3, 8, 128), F32),
            pltpu.VMEM((3, 3, 8, 128), F32),
            pltpu.VMEM((8, BLK), F32),
            pltpu.SemaphoreType.DMA((N_SEMS,)),
            pltpu.SemaphoreType.DMA((N_SEMS,)),
            pltpu.SemaphoreType.DMA((8,)),
        ],
        compiler_params=pltpu.CompilerParams(
            collective_id=0, has_side_effects=True, vmem_limit_bytes=60 * 2**20
        ),
    )(features, cotangent, weight)


def solution(mesh):
    in_specs = (P(("dp", "fsdp"), None), P(("dp", "fsdp"), None), P("fsdp", None))
    out_specs = P("fsdp", None)
    return jax.shard_map(body, mesh=mesh, in_specs=in_specs, out_specs=out_specs, check_vma=False)
```

time: 523 us -> 171 us (0.33)
  waiting for transfers between devices: 313 us -> 0 us
  Pallas kernels: 0 us -> 169 us
  blocking collectives: 109 us -> 0 us
  matrix products: 55.7 us -> 0 us
  local copies, waits for them, and re-layouts: 20.8 us -> 2.36 us
  between operations: 13.8 us -> 0.01 us
    pallas_call x0 -> x1, Pallas kernels: none -> 169 us  [body(): pl.pallas_call(kernel, out_shape=jax.ShapeDtypeStruct((ROWS, DO), F32), i...]
    reduce_scatter x2 -> x0, waiting for transfers between devices: 164 us -> none  [grad(): lax.psum_scatter(term.astype(jnp.bfloat16), 'fsdp', scatter_dimension=0,...]
    all_gather x3 -> x0, waiting for transfers between devices: 148 us -> none  [the longest x1 92.5 us: body(): feats = lax.all_gather(features, 'dp', axis=0, tiled=True)]
    psum x1 -> x0, blocking collectives: 65.9 us -> none  [body(): squares = lax.psum(jnp.sum(first * first), ('dp', 'fsdp'))]
    dot_general x2 -> x0, matrix products: 55.7 us -> none  [grad(): jnp.einsum('tr,tc->rc', feats, delta, preferred_element_type=jnp.float32)]
    all_to_all x1 -> x0, blocking collectives: 32.9 us -> none  [body(): lax.all_to_all(cotangent, 'dp', split_axis=1, concat_axis=0, tiled=True)]
    unnamed x3 -> x1, local copies, waits for them, and re-layouts: 16.3 us -> 2.36 us
    all_gather x1 -> x0, blocking collectives: 10.7 us -> none  [body(): return lax.all_gather(second, 'dp', axis=1, tiled=True).astype(jnp.float32)]
  transfers between devices with their start and end apart: 5 -> 0, of which waited for: 5 -> 0; matrix products, arithmetic and copies ran while one was open for 1% -> 0% of each run, Pallas kernels for 0% -> 0%
where the time goes in v2:
time: 171 us
  Pallas kernels  169 us (99%)
  local copies, waits for them, and re-layouts  2.36 us (1%)
    pallas_call x1, Pallas kernels, body(): pl.pallas_call(kernel, out_shape=jax.ShapeDtypeStruct((ROWS, DO), F32), i...  169 us

profile of v2, /device:TPU:1, one launch (start us, length us, event | category | flops | bytes accessed | tf_op | source)
XLA Modules:
  0.0 171.1 jit_solution(3677901984878171225)
XLA Ops:
  0.0 168.7 %shard_map.37 = f32[96,3072]{1,0:T(8,128)} custom-call(bf16[384,3072]{1,0:T(8,128)(2,1)} %feat.1, bf16[384,3072]{1,0:T(8,128)(2,1)} %cot.1, bf16[96,3072]{1,0:T(8,128)(2,1)} %weight.1), custom_call_target="tpu_custom_call" | custom-call | tf_op jit(solution)/shard_map/pallas_call | solution.py:434
  168.7 2.4 %copy.5 = f32[96,3072]{1,0:T(8,128)} copy(f32[96,3072]{1,0:T(8,128)} %shard_map.37) | data formatting | bytes 2359296

commit v3 on v2

v3 whole, which is shorter than its diff:
```python
import jax
import jax.numpy as jnp
from jax import lax
from jax.experimental import pallas as pl
from jax.experimental.pallas import tpu as pltpu
from jax.sharding import PartitionSpec as P

MESH = pl.DeviceIdType.MESH
F32 = jnp.float32
BF16 = jnp.bfloat16

RING = 4
TOK = 384
DI = 3072
DO = 3072
ROWS = 96
BLK = 256
NB = 3
SHARE = BLK * NB
PART = 128
PARTS = TOK // PART
N_SEMS = 256
ROOT = 0.7978845608028654
CUBIC = 0.044715
ORDER = (
    "aS0", "aS1", "aT0", "T1", "aT1", "F0", "aG0", "aS2", "G0", "aG1", "F1", "oA0", "oD0", "oG0", "aT2",
    "oA1", "oD1", "oG1", "G1", "F2", "aG2", "G2", "nA0", "nD0", "nG0", "rS0", "nA1", "nD1", "nG1", "rS1",
    "oA2", "oD2", "oG2", "rM0", "nA2", "nD2", "nG2", "rM1", "rT0", "rS2", "rT1", "rX0", "rM2", "rFirst0",
    "rX1", "bS0", "rT2", "rFirst1", "bT0", "bS1", "rX2", "bG0", "rFirst2", "N0", "bS2", "bT1", "N1", "pA0",
    "N2", "bT2", "pD0", "pG0", "bG1", "qS0", "bG2", "pA1", "qM0", "pD1", "pG1", "qS1", "pA2", "pD2", "qT0",
    "pG2", "qS2", "qM1", "qP0", "qC0", "qM2", "qT1", "qT2", "qP1", "qP2", "qC1", "qC2",
)


def kernel(
    feat, cot, weight, out,
    f, ft, c, d, v1, v2, a1, a2, g, r1, r2, t, tx, o, nown, nrecv, kvec,
    send_sems, recv_sems, local_sems,
):
    x = lax.axis_index("dp")
    ff = lax.axis_index("fsdp")
    z = ff // 8
    y = lax.rem(ff // 2, RING)
    core = lax.rem(ff, 2)
    s = 1 - 2 * core

    def wrap(v):
        return lax.rem(v + 2 * RING, RING)

    def dev(dx=0, dy=0, dz=0, other=False):
        cc = 1 - core if other else core
        return (wrap(x + dx), (wrap(z + dz) * RING + wrap(y + dy)) * 2 + cc)

    def ring_dev(axis, step):
        return dev(dy=step) if axis == "y" else dev(dz=step)

    counter = [0]
    pending = []

    def remote(src, dst, device):
        i = counter[0]
        counter[0] += 1
        cp = pltpu.make_async_remote_copy(
            src_ref=src, dst_ref=dst, send_sem=send_sems.at[i], recv_sem=recv_sems.at[i],
            device_id=device, device_id_type=MESH,
        )
        cp.start()
        pending.append(cp)
        return cp

    def drain():
        while pending:
            pending.pop().wait_send()

    def sent(copies):
        for cp in copies:
            cp.wait_send()
        pending[:] = [cp for cp in pending if not any(cp is other for other in copies)]

    local_counter = [0]

    def local(src, dst):
        i = local_counter[0]
        local_counter[0] += 1
        cp = pltpu.make_async_copy(src, dst, local_sems.at[i])
        cp.start()
        return cp

    def columns(dx, other, j):
        cc = 1 - core if other else core
        start = (lax.rem(x + dx + RING, 2) * 2 + cc) * SHARE + j * BLK
        return pl.ds(pl.multiple_of(start, BLK), BLK)

    def transpose(slot, part):
        @pl.loop(0, DI // BLK)
        def _(i):
            cols = pl.ds(pl.multiple_of(i * BLK, BLK), BLK)
            ft[cols, pl.ds(slot * TOK + part * PART, PART)] = f[slot, pl.ds(part * PART, PART), cols].T

    w_own = [local(weight.at[:, columns(0, False, j)], v1.at[j, z, y, core]) for j in range(NB)]
    f_own = local(feat, f.at[0])
    c_own = [local(cot.at[:, columns(0, False, j)], c.at[j, 0]) for j in range(NB)]

    barrier = pltpu.get_barrier_semaphore()
    norm_first = [dev(other=True), dev(dx=1), dev(dx=1, other=True)]
    norm_second = [dev(dy=n // RING, dz=n % RING) for n in range(1, RING * RING)]
    others = [dev(other=True)] + norm_second
    for step in (1, 2, 3):
        others += [dev(dx=step), dev(dx=step, other=True)]
    for other in others:
        pl.semaphore_signal(barrier, inc=1, device_id=other, device_id_type=MESH)
    f_own.wait()
    for k in range(PARTS):
        transpose(0, k)
    pl.semaphore_wait(barrier, len(others))

    sib = dev(other=True)
    w_sib = [
        remote(weight.at[:, columns(0, True, j)], v1.at[j, z, y, core], sib) for j in range(NB)
    ]
    f_x, c_x, c_xo = [], [], []

    def send_features(k):
        rows = pl.ds(k * PART, PART)
        f_x.append(remote(feat.at[rows], f.at[2, rows], dev(dx=s)))

    def send_cotangent(j):
        c_x.append(remote(cot.at[:, columns(1, False, j)], c.at[j, 2], dev(dx=s)))
        c_xo.append(remote(cot.at[:, columns(1, True, j)], c.at[j, 3], dev(dx=s, other=True)))

    for k in range(PARTS):
        send_features(k)
    for j in range(NB):
        send_cotangent(j)
    f_sib = remote(feat, f.at[1], sib)
    c_sib = [remote(cot.at[:, columns(0, True, j)], c.at[j, 1], sib) for j in range(NB)]

    class Gather:
        def __init__(self, v, j):
            self.v, self.j = v, j

        def piece(self, half, stage, step):
            axis = self.axis(half, stage)
            zz = wrap(z + step) if axis == "z" else z
            yy = wrap(y + step) if axis == "y" else y
            if stage == 1:
                return self.v.at[self.j, zz, yy, half]
            if axis == "z":
                return self.v.at[self.j, zz, :, half]
            return self.v.at[self.j, :, yy, half]

        def axis(self, half, stage):
            return ("y", "z")[(half + stage + 1) % 2]

        def start(self, stage):
            self.near, self.far, self.relay = {}, {}, {}
            self.direct = []
            for half in (0, 1):
                axis, own = self.axis(half, stage), self.piece(half, stage, 0)
                if stage == 1:
                    self.direct += [remote(own, own, ring_dev(axis, n)) for n in (1, 3, 2)]
                    continue
                self.near[half] = remote(own, own, ring_dev(axis, s))
                self.far[half] = remote(own, own, ring_dev(axis, -s))

        def forward(self, stage):
            for half in (0, 1):
                self.near[half].wait_recv()
                got = self.piece(half, stage, -s)
                self.relay[half] = remote(got, got, ring_dev(self.axis(half, stage), s))

        def finish(self, stage):
            for cp in self.direct:
                cp.wait_recv()
            for half in self.far:
                self.far[half].wait_recv()
                self.relay[half].wait_recv()

    class Scatter:
        def __init__(self, j):
            self.j = j
            self.first, self.back, self.merged, self.direct = {}, {}, {}, {}

        def axis(self, half, stage):
            return ("z", "y")[(half + stage + 1) % 2]

        def place(self, half, stage, step):
            axis = self.axis(half, stage)
            zz = wrap(z + step) if axis == "z" else z
            yy = wrap(y + step) if axis == "y" else y
            if stage == 2:
                return (self.j, zz, yy, half)
            if axis == "z":
                return (self.j, zz, slice(None), half)
            return (self.j, slice(None), yy, half)

        def land(self, half, stage, i):
            return (r1 if stage == 1 else r2).at[self.j, half, i]

        def copies(self):
            out = [cp for copies in self.direct.values() for cp in copies]
            return out + [*self.first.values(), *self.back.values(), *self.merged.values()]

        def start(self, stage):
            for half in (0, 1):
                axis = self.axis(half, stage)
                if stage == 2:
                    self.direct[half] = [
                        remote(
                            g.at[self.place(half, stage, n)], r2.at[self.j, half, n - 1], ring_dev(axis, n)
                        )
                        for n in (1, 3, 2)
                    ]
                    continue
                self.first[half] = remote(
                    g.at[self.place(half, stage, 2)], r1.at[self.j, half, 0], ring_dev(axis, s)
                )
                self.back[half] = remote(
                    g.at[self.place(half, stage, -s)], r1.at[self.j, half, 1], ring_dev(axis, -s)
                )

        def middle(self):
            for half in (0, 1):
                self.first[half].wait_recv()
                at = self.place(half, 1, s)
                g[at] = (g[at].astype(F32) + r1[self.j, half, 0].astype(F32)).astype(BF16)
                self.merged[half] = remote(
                    g.at[at], r1.at[self.j, half, 2], ring_dev(self.axis(half, 1), s)
                )

        def turn(self):
            for half in (0, 1):
                self.back[half].wait_recv()
                self.merged[half].wait_recv()
                at = self.place(half, 1, 0)
                total = g[at].astype(F32) + r1[self.j, half, 1].astype(F32) + r1[self.j, half, 2].astype(F32)
                g[at] = total.astype(BF16)
            self.start(2)

        def finish(self):
            for half in (0, 1):
                total = g[self.place(half, 2, 0)].astype(F32)
                for n, cp in enumerate(self.direct[half]):
                    cp.wait_recv()
                for n in range(3):
                    total = total + r2[self.j, half, n].astype(F32)
                t[self.j, half] = total.astype(BF16)

    def matmul(j, v, dst, lo, hi):
        product = jnp.dot(
            f[lo:hi].reshape((hi - lo) * TOK, DI), v[j].reshape(DI, BLK), preferred_element_type=F32
        )
        dst[lo:hi] = product.reshape(hi - lo, TOK, BLK)

    def delta(j, lo, hi, second):
        step = 64

        @pl.loop(lo, hi)
        def _(slot):
            @pl.loop(0, TOK // step)
            def _(i):
                rows = pl.ds(pl.multiple_of(i * step, step), step)
                a = a1[j, slot, rows, :]
                if second:
                    a = a + a2[slot, rows, :] * kvec[0:1, :]
                square = a * a
                th = jnp.tanh(ROOT * a * (1.0 + CUBIC * square))
                slope = 0.5 * (1.0 + th) + 0.5 * a * (1.0 - th * th) * (ROOT * (1.0 + 3.0 * CUBIC * square))
                scaled = c[j, slot, rows, :].astype(F32) * (1.0 / jnp.sqrt(F32(TOK * 128)))
                d[j, slot, rows, :] = (scaled * slope).astype(BF16)

    def grad(j, lo, hi, add):
        rows = DI // 2

        @pl.loop(0, 2)
        def _(i):
            left = ft[pl.ds(pl.multiple_of(i * rows, rows), rows), lo * TOK : hi * TOK]
            right = d[j, lo:hi].reshape((hi - lo) * TOK, BLK)
            term = jnp.dot(left, right, preferred_element_type=F32)
            at = (j, pl.ds(i * (RING // 2), RING // 2))
            if add:
                term = term + g[at].reshape(rows, BLK).astype(F32)
            g[at] = term.astype(BF16).reshape(RING // 2, RING, 2, ROWS, BLK)

    gather1 = [Gather(v1, j) for j in range(NB)]
    gather2 = [Gather(v2, j) for j in range(NB)]
    scatter1 = [Scatter(j) for j in range(NB)]
    scatter2 = [Scatter(j) for j in range(NB)]
    f_fwd, swap, share, state = {}, {}, {}, {}

    def weight_start(j):
        w_own[j].wait()
        w_sib[j].wait_recv()
        gather1[j].start(1)

    def gather_turn(ag):
        ag.finish(1)
        ag.start(2)

    def sibling_tokens():
        f_sib.wait_recv()
        for k in range(PARTS):
            transpose(1, k)

    def take_part(k):
        rows = pl.ds(k * PART, PART)
        f_x[k].wait_recv()
        f_fwd[k] = remote(f.at[2, rows], f.at[3, rows], sib)
        transpose(2, k)

    def take_forwarded(k):
        f_fwd[k].wait_recv()
        transpose(3, k)

    def own_act(j):
        gather1[j].finish(2)
        matmul(j, v1, a1.at[j], 0, 2)

    def own_delta(j):
        c_own[j].wait()
        c_sib[j].wait_recv()
        delta(j, 0, 2, False)

    def other_delta(j):
        c_x[j].wait_recv()
        c_xo[j].wait_recv()
        delta(j, 2, 4, False)

    def cross(j):
        scatter1[j].finish()
        swap[j] = remote(t.at[j], tx.at[j], dev(dx=2))

    def first(j):
        swap[j].wait_recv()
        total = t[j].astype(F32) + tx[j].astype(F32)
        v2[j, z, y] = total.astype(BF16)
        sq = (total * total).reshape(2 * ROWS // 8, 8, BLK).sum(axis=0)
        sq = sq[:, :128] + sq[:, 128:]
        nown[0] = sq if j == 0 else nown[0] + sq

    def norm_send(i, base, devices):
        state[i] = [remote(nown.at[i], nrecv.at[base + n], device) for n, device in enumerate(devices)]

    def norm_add(i, base):
        total = nown[i]
        for n, cp in enumerate(state[i]):
            cp.wait_recv()
            total = total + nrecv[base + n]
        return total

    def norm_start():
        norm_send(0, 0, norm_first)

    def norm_turn():
        nown[1] = norm_add(0, 0)
        norm_send(1, len(norm_first), norm_second)

    def norm_finish():
        total = jnp.sum(norm_add(1, len(norm_first)), keepdims=True)
        factor = 0.3 * jnp.sqrt(F32(DO)) / jnp.sqrt(total + 1e-06)
        kvec[...] = jnp.broadcast_to(factor, kvec.shape)

    def second_act(j):
        gather2[j].finish(2)
        matmul(j, v2, a2, 0, 4)

    def second_grad(j):
        sent(scatter1[j].copies())
        grad(j, 0, 4, False)

    def spread(j):
        sent([swap[j]])
        scatter2[j].finish()
        share[j] = [remote(t.at[j, 1 - core], o.at[j, 0, 1], sib)]
        for step in (2, 1, 3):
            share[j].append(remote(t.at[j, core], o.at[j, step, 0], dev(dx=step)))
            share[j].append(remote(t.at[j, 1 - core], o.at[j, step, 1], dev(dx=step, other=True)))

    def collect(j):
        for cp in share[j]:
            cp.wait_recv()
        for other in (False, True):
            same = t[j, core] if not other else o[j, 0, 1]
            k = int(other)
            out[:, columns(0, other, j)] = same.astype(F32) + o[j, 2, k].astype(F32)
            out[:, columns(1, other, j)] = o[j, 1, k].astype(F32) + o[j, 3, k].astype(F32)

    steps = {
        "aS": weight_start,
        "aT": lambda j: gather_turn(gather1[j]),
        "aG": lambda j: gather1[j].forward(2),
        "F": take_part,
        "G": take_forwarded,
        "oA": own_act,
        "oD": own_delta,
        "oG": lambda j: grad(j, 0, 2, False),
        "nA": lambda j: matmul(j, v1, a1.at[j], 2, 4),
        "nD": other_delta,
        "nG": lambda j: grad(j, 2, 4, True),
        "rS": lambda j: scatter1[j].start(1),
        "rM": lambda j: scatter1[j].middle(),
        "rT": lambda j: scatter1[j].turn(),
        "rX": cross,
        "rFirst": first,
        "bS": lambda j: gather2[j].start(1),
        "bT": lambda j: gather_turn(gather2[j]),
        "bG": lambda j: gather2[j].forward(2),
        "pA": second_act,
        "pD": lambda j: delta(j, 0, 4, True),
        "pG": second_grad,
        "qS": lambda j: scatter2[j].start(1),
        "qM": lambda j: scatter2[j].middle(),
        "qT": lambda j: scatter2[j].turn(),
        "qP": spread,
        "qC": collect,
    }
    single = {"T1": sibling_tokens, "N0": norm_start, "N1": norm_turn, "N2": norm_finish}
    for name in ORDER:
        if name in single:
            single[name]()
        else:
            steps[name[:-1]](int(name[-1]))
    drain()


def body(features, cotangent, weight):
    return pl.pallas_call(
        kernel,
        out_shape=jax.ShapeDtypeStruct((ROWS, DO), F32),
        in_specs=[pl.BlockSpec(memory_space=pl.ANY)] * 3,
        out_specs=pl.BlockSpec(memory_space=pltpu.VMEM),
        scratch_shapes=[
            pltpu.VMEM((4, TOK, DI), BF16),
            pltpu.VMEM((DI, 4 * TOK), BF16),
            pltpu.VMEM((NB, 4, TOK, BLK), BF16),
            pltpu.VMEM((NB, 4, TOK, BLK), BF16),
            pltpu.VMEM((NB, RING, RING, 2, ROWS, BLK), BF16),
            pltpu.VMEM((NB, RING, RING, 2, ROWS, BLK), BF16),
            pltpu.VMEM((NB, 4, TOK, BLK), F32),
            pltpu.VMEM((4, TOK, BLK), F32),
            pltpu.VMEM((NB, RING, RING, 2, ROWS, BLK), BF16),
            pltpu.VMEM((NB, 2, 3, RING, ROWS, BLK), BF16),
            pltpu.VMEM((NB, 2, 3, ROWS, BLK), BF16),
            pltpu.VMEM((NB, 2, ROWS, BLK), BF16),
            pltpu.VMEM((NB, 2, ROWS, BLK), BF16),
            pltpu.VMEM((NB, 4, 2, ROWS, BLK), BF16),
            pltpu.VMEM((2, 8, 128), F32),
            pltpu.VMEM((18, 8, 128), F32),
            pltpu.VMEM((8, BLK), F32),
            pltpu.SemaphoreType.DMA((N_SEMS,)),
            pltpu.SemaphoreType.DMA((N_SEMS,)),
            pltpu.SemaphoreType.DMA((8,)),
        ],
        compiler_params=pltpu.CompilerParams(
            collective_id=0, has_side_effects=True, vmem_limit_bytes=60 * 2**20
        ),
    )(features, cotangent, weight)


def solution(mesh):
    in_specs = (P(("dp", "fsdp"), None), P(("dp", "fsdp"), None), P("fsdp", None))
    out_specs = P("fsdp", None)
    return jax.shard_map(body, mesh=mesh, in_specs=in_specs, out_specs=out_specs, check_vma=False)
```

time: 171 us -> 152 us (0.89)
  Pallas kernels: 169 us -> 149 us
    pallas_call x1, Pallas kernels: 169 us -> 149 us  [body(): pl.pallas_call(kernel, out_shape=jax.ShapeDtypeStruct((ROWS, DO), F32), i...]
where the time goes in v3:
time: 152 us
  Pallas kernels  149 us (98%)
  local copies, waits for them, and re-layouts  2.36 us (2%)
    pallas_call x1, Pallas kernels, body(): pl.pallas_call(kernel, out_shape=jax.ShapeDtypeStruct((ROWS, DO), F32), i...  149 us

profile of v3, /device:TPU:1, one launch (start us, length us, event | category | flops | bytes accessed | tf_op | source)
XLA Modules:
  0.0 151.7 jit_solution(10096307764190551181)
XLA Ops:
  0.0 149.3 %shard_map.37 = f32[96,3072]{1,0:T(8,128)} custom-call(bf16[384,3072]{1,0:T(8,128)(2,1)} %feat.1, bf16[384,3072]{1,0:T(8,128)(2,1)} %cot.1, bf16[96,3072]{1,0:T(8,128)(2,1)} %weight.1), custom_call_target="tpu_custom_call" | custom-call | tf_op jit(solution)/shard_map/pallas_call | solution.py:427
  149.3 2.4 %copy.5 = f32[96,3072]{1,0:T(8,128)} copy(f32[96,3072]{1,0:T(8,128)} %shard_map.37) | data formatting | bytes 2359296

commit v4 on v3

v4 whole, which is shorter than its diff:
```python
import jax
import jax.numpy as jnp
from jax import lax
from jax.experimental import pallas as pl
from jax.experimental.pallas import tpu as pltpu
from jax.sharding import PartitionSpec as P

MESH = pl.DeviceIdType.MESH
F32 = jnp.float32
BF16 = jnp.bfloat16

RING = 4
TOK = 384
DI = 3072
DO = 3072
ROWS = 96
BLK = 256
NB = 3
SHARE = BLK * NB
PART = 128
PARTS = TOK // PART
N_SEMS = 45
LOW, HIGH = slice(0, RING // 2), slice(RING // 2, RING)
ROOT = 0.7978845608028654
CUBIC = 0.044715
ORDER = (
    "aS0", "aT0", "aS1", "T1", "aG0", "aS2", "F0", "G0", "aT1", "oA0", "oD0", "oG0", "F1", "aT2", "aG1", "G1",
    "aG2", "F2", "oA1", "G2", "nA0", "nD0", "nG0", "rS0", "nA1", "nD1", "oD1", "oG1", "rM0", "nG1", "rS1",
    "oA2", "oD2", "oG2", "rT0", "rM1", "nA2", "nD2", "nG2", "rS2", "rX0", "rT1", "rM2", "rFirst0", "bS0",
    "rX1", "rT2", "bT0", "rFirst1", "bS1", "rX2", "bG0", "rFirst2", "N0", "bS2", "bT1", "N1", "pA0", "N2",
    "pD0", "bT2", "pG0", "bG1", "qS0", "bG2", "pA1", "qM0", "pD1", "pG1", "qS1", "pA2", "qT0", "pD2", "pG2",
    "qS2", "qM1", "qP0", "qM2", "qC0", "qT1", "qT2", "qP1", "qP2", "qC1", "qC2",
)


def kernel(
    feat, cot, weight, out,
    f, ft, c, d, v1, v2, a1, a2, g, r1, r2, t, tx, o, nown, nrecv, kvec,
    send_sems, recv_sems, local_sems,
):
    x = lax.axis_index("dp")
    ff = lax.axis_index("fsdp")
    z = ff // 8
    y = lax.rem(ff // 2, RING)
    core = lax.rem(ff, 2)
    s = 1 - 2 * core

    def wrap(v):
        return lax.rem(v + 2 * RING, RING)

    def dev(dx=0, dy=0, dz=0, other=False):
        cc = 1 - core if other else core
        return (wrap(x + dx), (wrap(z + dz) * RING + wrap(y + dy)) * 2 + cc)

    def ring_dev(axis, step):
        return dev(dy=step) if axis == "y" else dev(dz=step)

    counter = [0]
    pending = []

    class Group:
        def __init__(self, like, again=None):
            self.like = like
            if again is None:
                self.i = counter[0]
                counter[0] += 1
            else:
                self.i = again.i

        def send(self, src, dst, device):
            if not any(group is self for group in pending):
                pending.append(self)
            pltpu.make_async_remote_copy(
                src_ref=src, dst_ref=dst, send_sem=send_sems.at[self.i], recv_sem=recv_sems.at[self.i],
                device_id=device, device_id_type=MESH,
            ).start()

        def wait_recv(self):
            pltpu.make_async_copy(self.like, self.like, recv_sems.at[self.i]).wait()

        def wait_send(self):
            pltpu.make_async_copy(self.like, self.like, send_sems.at[self.i]).wait()
            pending[:] = [group for group in pending if group is not self]

    def remote(src, dst, device):
        group = Group(dst)
        group.send(src, dst, device)
        return group

    def drain():
        for group in list(pending):
            group.wait_send()

    def sent(groups):
        for group in groups:
            group.wait_send()

    local_counter = [0]

    def local(src, dst):
        i = local_counter[0]
        local_counter[0] += 1
        cp = pltpu.make_async_copy(src, dst, local_sems.at[i])
        cp.start()
        return cp

    def columns(dx, other, j):
        cc = 1 - core if other else core
        start = (lax.rem(x + dx + RING, 2) * 2 + cc) * SHARE + j * BLK
        return pl.ds(pl.multiple_of(start, BLK), BLK)

    def transpose(slot, part):
        @pl.loop(0, DI // BLK)
        def _(i):
            cols = pl.ds(pl.multiple_of(i * BLK, BLK), BLK)
            ft[cols, pl.ds(slot * TOK + part * PART, PART)] = f[slot, pl.ds(part * PART, PART), cols].T

    barrier = pltpu.get_barrier_semaphore()
    norm_first = [dev(other=True), dev(dx=1), dev(dx=1, other=True)]
    norm_second = [dev(dy=n // RING, dz=n % RING) for n in range(1, RING * RING)]
    others = [dev(other=True)] + norm_second
    for step in (1, 2, 3):
        others += [dev(dx=step), dev(dx=step, other=True)]
    for other in others:
        pl.semaphore_signal(barrier, inc=1, device_id=other, device_id_type=MESH)
    w_own = [local(weight.at[:, columns(0, False, j)], v1.at[j, z, y, core]) for j in range(NB)]
    f_own = local(feat, f.at[0])
    c_own = [local(cot.at[:, columns(0, False, j)], c.at[j, 0]) for j in range(NB)]
    pl.semaphore_wait(barrier, len(others))

    sib = dev(other=True)
    f_x, c_x = [], []

    def send_features(k):
        rows = pl.ds(k * PART, PART)
        f_x.append(remote(feat.at[rows], f.at[2, rows], dev(dx=s)))

    def send_cotangent(j):
        c_x.append(Group(c.at[j, 2:4]))
        c_x[j].send(cot.at[:, columns(1, False, j)], c.at[j, 2], dev(dx=s))
        c_x[j].send(cot.at[:, columns(1, True, j)], c.at[j, 3], dev(dx=s, other=True))

    for k in range(PARTS):
        send_features(k)
    for j in range(NB):
        send_cotangent(j)
    w_sib = [
        remote(weight.at[:, columns(0, True, j)], v1.at[j, z, y, core], sib) for j in range(NB)
    ]
    f_sib = remote(feat, f.at[1], sib)
    c_sib = [remote(cot.at[:, columns(0, True, j)], c.at[j, 1], sib) for j in range(NB)]

    f_own.wait()
    for k in range(PARTS):
        transpose(0, k)

    class Gather:
        def __init__(self, v, j, again=None):
            self.v, self.j = v, j
            likes = (v.at[j, 0, 0:3], v.at[j, 0], v.at[j, 0:2])
            self.groups = [Group(like, again and again.groups[i]) for i, like in enumerate(likes)]
            self.direct, self.early, self.late = self.groups

        def axis(self, half, stage):
            return ("y", "z")[(half + stage + 1) % 2]

        def piece(self, half, stage, step, part=None):
            axis = self.axis(half, stage)
            zz = wrap(z + step) if axis == "z" else z
            yy = wrap(y + step) if axis == "y" else y
            if stage == 1:
                return self.v.at[self.j, zz, yy, half]
            if axis == "z":
                return self.v.at[self.j, zz, part, half]
            return self.v.at[self.j, part, yy, half]

        def start(self):
            for half in (0, 1):
                own, axis = self.piece(half, 1, 0), self.axis(half, 1)
                for n in (1, 3, 2):
                    self.direct.send(own, own, ring_dev(axis, n))

        def turn(self):
            self.direct.wait_recv()
            for group, parts in ((self.early, (LOW, HIGH)), (self.late, (HIGH, LOW))):
                for step, part in zip((1, -1), parts):
                    for half in (0, 1):
                        own = self.piece(half, 2, 0, part)
                        group.send(own, own, ring_dev(self.axis(half, 2), step))

        def forward(self):
            self.early.wait_recv()
            for step, part in ((1, LOW), (-1, HIGH)):
                for half in (0, 1):
                    got = self.piece(half, 2, -step, part)
                    self.late.send(got, got, ring_dev(self.axis(half, 2), step))

        def finish(self):
            self.late.wait_recv()

    class Scatter:
        def __init__(self, j, again=None):
            self.j = j
            likes = (r1.at[j, :, 0], r1.at[j, :, 1:3], r2.at[j])
            self.groups = [Group(like, again and again.groups[i]) for i, like in enumerate(likes)]
            self.far, self.near, self.direct = self.groups

        def axis(self, half, stage):
            return ("z", "y")[(half + stage + 1) % 2]

        def place(self, half, stage, step, part=slice(None)):
            axis = self.axis(half, stage)
            zz = wrap(z + step) if axis == "z" else z
            yy = wrap(y + step) if axis == "y" else y
            if stage == 2:
                return (self.j, zz, yy, half)
            if axis == "z":
                return (self.j, zz, part, half)
            return (self.j, part, yy, half)

        def send(self, group, half, step, to, part, land):
            group.send(
                g.at[self.place(half, 1, step, part)], r1.at[self.j, half, land, part], ring_dev(self.axis(half, 1), to)
            )

        def start(self):
            for step, part in ((1, LOW), (-1, HIGH)):
                for half in (0, 1):
                    self.send(self.far, half, 2, step, part, 0)
            for step, part, land in ((1, HIGH, 1), (-1, LOW, 2)):
                for half in (0, 1):
                    self.send(self.near, half, step, step, part, land)

        def middle(self):
            self.far.wait_recv()
            for step, part, land in ((1, LOW, 1), (-1, HIGH, 2)):
                for half in (0, 1):
                    at = self.place(half, 1, step, part)
                    g[at] = (g[at].astype(F32) + r1[self.j, half, 0, part].astype(F32)).astype(BF16)
                    self.send(self.near, half, step, step, part, land)

        def turn(self):
            self.near.wait_recv()
            for half in (0, 1):
                at = self.place(half, 1, 0)
                total = g[at].astype(F32) + r1[self.j, half, 1].astype(F32) + r1[self.j, half, 2].astype(F32)
                g[at] = total.astype(BF16)
                for n in (1, 3, 2):
                    self.direct.send(
                        g.at[self.place(half, 2, n)], r2.at[self.j, half, n - 1], ring_dev(self.axis(half, 2), n)
                    )

        def finish(self):
            self.direct.wait_recv()
            for half in (0, 1):
                total = g[self.place(half, 2, 0)].astype(F32)
                for n in range(3):
                    total = total + r2[self.j, half, n].astype(F32)
                t[self.j, half] = total.astype(BF16)

    def matmul(j, v, dst, lo, hi):
        @pl.loop(lo, hi)
        def _(slot):
            dst[slot] = jnp.dot(f[slot], v[j].reshape(DI, BLK), preferred_element_type=F32)

    def delta(j, lo, hi, second):
        step = 64

        @pl.loop(lo, hi)
        def _(slot):
            @pl.loop(0, TOK // step)
            def _(i):
                rows = pl.ds(pl.multiple_of(i * step, step), step)
                a = a1[j, slot, rows, :]
                if second:
                    a = a + a2[slot, rows, :] * kvec[0:1, :]
                square = a * a
                th = jnp.tanh(ROOT * a * (1.0 + CUBIC * square))
                slope = 0.5 * (1.0 + th) + 0.5 * a * (1.0 - th * th) * (ROOT * (1.0 + 3.0 * CUBIC * square))
                scaled = c[j, slot, rows, :].astype(F32) * (1.0 / jnp.sqrt(F32(TOK * 128)))
                d[j, slot, rows, :] = (scaled * slope).astype(BF16)

    def grad(j, lo, hi, add):
        rows = DI // 4

        @pl.loop(0, 4)
        def _(i):
            left = ft[pl.ds(pl.multiple_of(i * rows, rows), rows), lo * TOK : hi * TOK]
            right = d[j, lo:hi].reshape((hi - lo) * TOK, BLK)
            term = jnp.dot(left, right, preferred_element_type=F32)
            at = (j, pl.ds(i, 1))
            if add:
                term = term + g[at].reshape(rows, BLK).astype(F32)
            g[at] = term.astype(BF16).reshape(1, RING, 2, ROWS, BLK)

    gather1 = [Gather(v1, j) for j in range(NB)]
    gather2 = [Gather(v2, j, gather1[j]) for j in range(NB)]
    scatter1 = [Scatter(j) for j in range(NB)]
    scatter2 = [Scatter(j, scatter1[j]) for j in range(NB)]
    f_fwd, swap, share, state = {}, {}, {}, {}

    def weight_start(j):
        w_own[j].wait()
        w_sib[j].wait_recv()
        gather1[j].start()

    def sibling_tokens():
        f_sib.wait_recv()
        for k in range(PARTS):
            transpose(1, k)

    def take_part(k):
        rows = pl.ds(k * PART, PART)
        f_x[k].wait_recv()
        f_fwd[k] = remote(f.at[2, rows], f.at[3, rows], sib)
        transpose(2, k)

    def take_forwarded(k):
        f_fwd[k].wait_recv()
        transpose(3, k)

    def own_act(j):
        gather1[j].finish()
        matmul(j, v1, a1.at[j], 0, 2)

    def own_delta(j):
        c_own[j].wait()
        c_sib[j].wait_recv()
        delta(j, 0, 2, False)

    def other_delta(j):
        c_x[j].wait_recv()
        delta(j, 2, 4, False)

    def gather_start(j):
        sent(gather1[j].groups)
        gather2[j].start()

    def cross(j):
        scatter1[j].finish()
        swap[j] = remote(t.at[j], tx.at[j], dev(dx=2))

    def first(j):
        swap[j].wait_recv()
        total = t[j].astype(F32) + tx[j].astype(F32)
        v2[j, z, y] = total.astype(BF16)
        sq = (total * total).reshape(2 * ROWS // 8, 8, BLK).sum(axis=0)
        sq = sq[:, :128] + sq[:, 128:]
        nown[0] = sq if j == 0 else nown[0] + sq

    def norm_send(i, base, devices):
        state[i] = Group(nrecv.at[base : base + len(devices)])
        for n, device in enumerate(devices):
            state[i].send(nown.at[i], nrecv.at[base + n], device)

    def norm_add(i, base, count):
        state[i].wait_recv()
        return nown[i] + nrecv[base : base + count].sum(axis=0)

    def norm_start():
        norm_send(0, 0, norm_first)

    def norm_turn():
        nown[1] = norm_add(0, 0, len(norm_first))
        norm_send(1, len(norm_first), norm_second)

    def norm_finish():
        total = jnp.sum(norm_add(1, len(norm_first), len(norm_second)), keepdims=True)
        factor = 0.3 * jnp.sqrt(F32(DO)) / jnp.sqrt(total + 1e-06)
        kvec[...] = jnp.broadcast_to(factor, kvec.shape)

    def second_act(j):
        gather2[j].finish()
        matmul(j, v2, a2, 0, 4)

    def second_grad(j):
        sent(scatter1[j].groups)
        grad(j, 0, 4, False)

    def spread(j):
        sent([swap[j]])
        scatter2[j].finish()
        far = Group(o.at[j, 1:4])
        for step in (2, 1, 3):
            far.send(t.at[j, core], o.at[j, step, 0], dev(dx=step))
            far.send(t.at[j, 1 - core], o.at[j, step, 1], dev(dx=step, other=True))
        share[j] = [far, remote(t.at[j, 1 - core], o.at[j, 0, 1], sib)]

    def collect(j):
        for cp in share[j]:
            cp.wait_recv()
        for other in (False, True):
            same = t[j, core] if not other else o[j, 0, 1]
            k = int(other)
            out[:, columns(0, other, j)] = same.astype(F32) + o[j, 2, k].astype(F32)
            out[:, columns(1, other, j)] = o[j, 1, k].astype(F32) + o[j, 3, k].astype(F32)

    steps = {
        "aS": weight_start,
        "aT": lambda j: gather1[j].turn(),
        "aG": lambda j: gather1[j].forward(),
        "F": take_part,
        "G": take_forwarded,
        "oA": own_act,
        "oD": own_delta,
        "oG": lambda j: grad(j, 0, 2, False),
        "nA": lambda j: matmul(j, v1, a1.at[j], 2, 4),
        "nD": other_delta,
        "nG": lambda j: grad(j, 2, 4, True),
        "rS": lambda j: scatter1[j].start(),
        "rM": lambda j: scatter1[j].middle(),
        "rT": lambda j: scatter1[j].turn(),
        "rX": cross,
        "rFirst": first,
        "bS": gather_start,
        "bT": lambda j: gather2[j].turn(),
        "bG": lambda j: gather2[j].forward(),
        "pA": second_act,
        "pD": lambda j: delta(j, 0, 4, True),
        "pG": second_grad,
        "qS": lambda j: scatter2[j].start(),
        "qM": lambda j: scatter2[j].middle(),
        "qT": lambda j: scatter2[j].turn(),
        "qP": spread,
        "qC": collect,
    }
    single = {"T1": sibling_tokens, "N0": norm_start, "N1": norm_turn, "N2": norm_finish}
    for name in ORDER:
        if name in single:
            single[name]()
        else:
            steps[name[:-1]](int(name[-1]))
    drain()


def body(features, cotangent, weight):
    return pl.pallas_call(
        kernel,
        out_shape=jax.ShapeDtypeStruct((ROWS, DO), F32),
        in_specs=[pl.BlockSpec(memory_space=pl.ANY)] * 3,
        out_specs=pl.BlockSpec(memory_space=pltpu.VMEM),
        scratch_shapes=[
            pltpu.VMEM((4, TOK, DI), BF16),
            pltpu.VMEM((DI, 4 * TOK), BF16),
            pltpu.VMEM((NB, 4, TOK, BLK), BF16),
            pltpu.VMEM((NB, 4, TOK, BLK), BF16),
            pltpu.VMEM((NB, RING, RING, 2, ROWS, BLK), BF16),
            pltpu.VMEM((NB, RING, RING, 2, ROWS, BLK), BF16),
            pltpu.VMEM((NB, 4, TOK, BLK), F32),
            pltpu.VMEM((4, TOK, BLK), F32),
            pltpu.VMEM((NB, RING, RING, 2, ROWS, BLK), BF16),
            pltpu.VMEM((NB, 2, 3, RING, ROWS, BLK), BF16),
            pltpu.VMEM((NB, 2, 3, ROWS, BLK), BF16),
            pltpu.VMEM((NB, 2, ROWS, BLK), BF16),
            pltpu.VMEM((NB, 2, ROWS, BLK), BF16),
            pltpu.VMEM((NB, 4, 2, ROWS, BLK), BF16),
            pltpu.VMEM((2, 8, 128), F32),
            pltpu.VMEM((18, 8, 128), F32),
            pltpu.VMEM((8, BLK), F32),
            pltpu.SemaphoreType.DMA((N_SEMS,)),
            pltpu.SemaphoreType.DMA((N_SEMS,)),
            pltpu.SemaphoreType.DMA((8,)),
        ],
        compiler_params=pltpu.CompilerParams(
            collective_id=0, has_side_effects=True, vmem_limit_bytes=60 * 2**20
        ),
    )(features, cotangent, weight)


def solution(mesh):
    in_specs = (P(("dp", "fsdp"), None), P(("dp", "fsdp"), None), P("fsdp", None))
    out_specs = P("fsdp", None)
    return jax.shard_map(body, mesh=mesh, in_specs=in_specs, out_specs=out_specs, check_vma=False)
```

time: 152 us -> 145 us (0.954)
  Pallas kernels: 149 us -> 142 us
    pallas_call x1, Pallas kernels: 149 us -> 142 us  [body(): pl.pallas_call(kernel, out_shape=jax.ShapeDtypeStruct((ROWS, DO), F32), i...]
where the time goes in v4:
time: 145 us; the launch traced here: 144 us
  Pallas kernels  142 us (98%)
  local copies, waits for them, and re-layouts  2.36 us (2%)
    pallas_call x1, Pallas kernels, body(): pl.pallas_call(kernel, out_shape=jax.ShapeDtypeStruct((ROWS, DO), F32), i...  142 us

profile of v4, /device:TPU:1, one launch (start us, length us, event | category | flops | bytes accessed | tf_op | source)
XLA Modules:
  0.0 144.4 jit_solution(6537329542974243647)
XLA Ops:
  0.0 142.0 %shard_map.37 = f32[96,3072]{1,0:T(8,128)} custom-call(bf16[384,3072]{1,0:T(8,128)(2,1)} %feat.1, bf16[384,3072]{1,0:T(8,128)(2,1)} %cot.1, bf16[96,3072]{1,0:T(8,128)(2,1)} %weight.1), custom_call_target="tpu_custom_call" | custom-call | tf_op jit(solution)/shard_map/pallas_call | solution.py:437
  142.0 2.4 %copy.5 = f32[96,3072]{1,0:T(8,128)} copy(f32[96,3072]{1,0:T(8,128)} %shard_map.37) | data formatting | bytes 2359296

commit v5 on v4

--- a/solution.py
+++ b/solution.py
@@ -19,23 +19,23 @@
 SHARE = BLK * NB
 PART = 128
 PARTS = TOK // PART
-N_SEMS = 45
+N_SEMS = 46
 LOW, HIGH = slice(0, RING // 2), slice(RING // 2, RING)
 ROOT = 0.7978845608028654
 CUBIC = 0.044715
 ORDER = (
     "aS0", "aT0", "aS1", "T1", "aG0", "aS2", "F0", "G0", "aT1", "oA0", "oD0", "oG0", "F1", "aT2", "aG1", "G1",
-    "aG2", "F2", "oA1", "G2", "nA0", "nD0", "nG0", "rS0", "nA1", "nD1", "oD1", "oG1", "rM0", "nG1", "rS1",
+    "aG2", "F2", "G2", "nA0", "nD0", "nG0", "rS0", "oA1", "oD1", "oG1", "nA1", "nD1", "rM0", "nG1", "rS1",
     "oA2", "oD2", "oG2", "rT0", "rM1", "nA2", "nD2", "nG2", "rS2", "rX0", "rT1", "rM2", "rFirst0", "bS0",
-    "rX1", "rT2", "bT0", "rFirst1", "bS1", "rX2", "bG0", "rFirst2", "N0", "bS2", "bT1", "N1", "pA0", "N2",
-    "pD0", "bT2", "pG0", "bG1", "qS0", "bG2", "pA1", "qM0", "pD1", "pG1", "qS1", "pA2", "qT0", "pD2", "pG2",
-    "qS2", "qM1", "qP0", "qM2", "qC0", "qT1", "qT2", "qP1", "qP2", "qC1", "qC2",
+    "rX1", "rT2", "bT0", "rFirst1", "bS1", "rX2", "bG0", "rFirst2", "N0", "bS2", "N1", "bT1", "N2", "pA0",
+    "N3", "bT2", "pD0", "pG0", "bG1", "qS0", "bG2", "pA1", "qM0", "pD1", "pG1", "qS1", "pA2", "qT0", "pD2",
+    "pG2", "qS2", "qM1", "qP0", "qM2", "qC0", "qT1", "qT2", "qP1", "qP2", "qC1", "qC2",
 )
 
 
 def kernel(
     feat, cot, weight, out,
-    f, ft, c, d, v1, v2, a1, a2, g, r1, r2, t, tx, o, nown, nrecv, kvec,
+    f, ft, c, d, v1, v2, a1, a2, g, r1, r2, t, tx, o, nown, nrecv, kvec, result,
     send_sems, recv_sems, local_sems,
 ):
     x = lax.axis_index("dp")
@@ -117,10 +117,10 @@
 
     barrier = pltpu.get_barrier_semaphore()
     norm_first = [dev(other=True), dev(dx=1), dev(dx=1, other=True)]
-    norm_second = [dev(dy=n // RING, dz=n % RING) for n in range(1, RING * RING)]
-    others = [dev(other=True)] + norm_second
+    norm_rings = (norm_first, [dev(dy=n) for n in (1, 2, 3)], [dev(dz=n) for n in (1, 2, 3)])
+    others = [dev(other=True)]
     for step in (1, 2, 3):
-        others += [dev(dx=step), dev(dx=step, other=True)]
+        others += [dev(dx=step), dev(dx=step, other=True), dev(dy=step), dev(dz=step)]
     for other in others:
         pl.semaphore_signal(barrier, inc=1, device_id=other, device_id_type=MESH)
     w_own = [local(weight.at[:, columns(0, False, j)], v1.at[j, z, y, core]) for j in range(NB)]
@@ -298,6 +298,7 @@
     scatter1 = [Scatter(j) for j in range(NB)]
     scatter2 = [Scatter(j, scatter1[j]) for j in range(NB)]
     f_fwd, swap, share, state = {}, {}, {}, {}
+    written = []
 
     def weight_start(j):
         w_own[j].wait()
@@ -348,24 +349,21 @@
         sq = sq[:, :128] + sq[:, 128:]
         nown[0] = sq if j == 0 else nown[0] + sq
 
-    def norm_send(i, base, devices):
-        state[i] = Group(nrecv.at[base : base + len(devices)])
-        for n, device in enumerate(devices):
-            state[i].send(nown.at[i], nrecv.at[base + n], device)
-
-    def norm_add(i, base, count):
+    def norm_send(i):
+        state[i] = Group(nrecv.at[i])
+        for n, device in enumerate(norm_rings[i]):
+            state[i].send(nown.at[i], nrecv.at[i, n], device)
+
+    def norm_add(i):
         state[i].wait_recv()
-        return nown[i] + nrecv[base : base + count].sum(axis=0)
-
-    def norm_start():
-        norm_send(0, 0, norm_first)
-
-    def norm_turn():
-        nown[1] = norm_add(0, 0, len(norm_first))
-        norm_send(1, len(norm_first), norm_second)
+        return nown[i] + nrecv[i, 0] + nrecv[i, 1] + nrecv[i, 2]
+
+    def norm_turn(i):
+        nown[i] = norm_add(i - 1)
+        norm_send(i)
 
     def norm_finish():
-        total = jnp.sum(norm_add(1, len(norm_first), len(norm_second)), keepdims=True)
+        total = jnp.sum(norm_add(2), keepdims=True)
         factor = 0.3 * jnp.sqrt(F32(DO)) / jnp.sqrt(total + 1e-06)
         kvec[...] = jnp.broadcast_to(factor, kvec.shape)
 
@@ -392,8 +390,11 @@
         for other in (False, True):
             same = t[j, core] if not other else o[j, 0, 1]
             k = int(other)
-            out[:, columns(0, other, j)] = same.astype(F32) + o[j, 2, k].astype(F32)
-            out[:, columns(1, other, j)] = o[j, 1, k].astype(F32) + o[j, 3, k].astype(F32)
+            result[j, 0, k] = (same.astype(F32) + o[j, 2, k].astype(F32)).astype(BF16)
+            result[j, 1, k] = (o[j, 1, k].astype(F32) + o[j, 3, k].astype(F32)).astype(BF16)
+        for parity in (0, 1):
+            for k in (0, 1):
+                written.append(local(result.at[j, parity, k], out.at[:, columns(parity, k == 1, j)]))
 
     steps = {
         "aS": weight_start,
@@ -424,21 +425,29 @@
         "qP": spread,
         "qC": collect,
     }
-    single = {"T1": sibling_tokens, "N0": norm_start, "N1": norm_turn, "N2": norm_finish}
+    single = {
+        "T1": sibling_tokens,
+        "N0": lambda: norm_send(0),
+        "N1": lambda: norm_turn(1),
+        "N2": lambda: norm_turn(2),
+        "N3": norm_finish,
+    }
     for name in ORDER:
         if name in single:
             single[name]()
         else:
             steps[name[:-1]](int(name[-1]))
     drain()
+    for cp in written:
+        cp.wait()
 
 
 def body(features, cotangent, weight):
     return pl.pallas_call(
         kernel,
-        out_shape=jax.ShapeDtypeStruct((ROWS, DO), F32),
+        out_shape=jax.ShapeDtypeStruct((ROWS, DO), BF16),
         in_specs=[pl.BlockSpec(memory_space=pl.ANY)] * 3,
-        out_specs=pl.BlockSpec(memory_space=pltpu.VMEM),
+        out_specs=pl.BlockSpec(memory_space=pl.ANY),
         scratch_shapes=[
             pltpu.VMEM((4, TOK, DI), BF16),
             pltpu.VMEM((DI, 4 * TOK), BF16),
@@ -454,17 +463,18 @@
             pltpu.VMEM((NB, 2, ROWS, BLK), BF16),
             pltpu.VMEM((NB, 2, ROWS, BLK), BF16),
             pltpu.VMEM((NB, 4, 2, ROWS, BLK), BF16),
-            pltpu.VMEM((2, 8, 128), F32),
-            pltpu.VMEM((18, 8, 128), F32),
+            pltpu.VMEM((3, 8, 128), F32),
+            pltpu.VMEM((3, 3, 8, 128), F32),
             pltpu.VMEM((8, BLK), F32),
+            pltpu.VMEM((NB, 2, 2, ROWS, BLK), BF16),
             pltpu.SemaphoreType.DMA((N_SEMS,)),
             pltpu.SemaphoreType.DMA((N_SEMS,)),
-            pltpu.SemaphoreType.DMA((8,)),
+            pltpu.SemaphoreType.DMA((19,)),
         ],
         compiler_params=pltpu.CompilerParams(
             collective_id=0, has_side_effects=True, vmem_limit_bytes=60 * 2**20
         ),
-    )(features, cotangent, weight)
+    )(features, cotangent, weight).astype(F32)
 
 
 def solution(mesh):

time: 145 us -> 142 us (0.979)
  local copies, waits for them, and re-layouts: 2.36 us -> 0 us
  other arithmetic: 0 us -> 2.18 us
  Pallas kernels: 142 us -> 140 us
    unnamed x1 -> x0, local copies, waits for them, and re-layouts: 2.36 us -> none
    pallas_call x1, Pallas kernels: 142 us -> 140 us  [body(): pl.pallas_call(kernel, out_shape=jax.ShapeDtypeStruct((ROWS, DO), BF16),...]
    convert_element_type x0 -> x1, other arithmetic: none -> 2.18 us  [body(): return pl.pallas_call(kernel, out_shape=jax.ShapeDtypeStruct((ROWS, DO),...]
where the time goes in v5:
time: 142 us
  Pallas kernels  140 us (99%)
  other arithmetic  2.18 us (2%)
    pallas_call x1, Pallas kernels, body(): pl.pallas_call(kernel, out_shape=jax.ShapeDtypeStruct((ROWS, DO), BF16),...  140 us

profile of v5, /device:TPU:1, one launch (start us, length us, event | category | flops | bytes accessed | tf_op | source)
XLA Modules:
  0.0 141.9 jit_solution(15549086837335754032)
XLA Ops:
  0.0 139.7 %shard_map.37 = bf16[96,3072]{1,0:T(8,128)(2,1)} custom-call(bf16[384,3072]{1,0:T(8,128)(2,1)} %feat.1, bf16[384,3072]{1,0:T(8,128)(2,1)} %cot.1, bf16[96,3072]{1,0:T(8,128)(2,1)} %weight.1), custom_call_target="tpu_custom_call" | custom-call | tf_op jit(solution)/shard_map/pallas_call | solution.py:446
  139.7 2.2 %convert_element_type.3 = f32[96,3072]{1,0:T(8,128)} convert(bf16[96,3072]{1,0:T(8,128)(2,1)} %shard_map.37) | non-fusion elementwise | flops 294912 | bytes 1769472 | tf_op jit(solution)/shard_map/convert_element_type | solution.py:477

commit v6 on v5

--- a/solution.py
+++ b/solution.py
@@ -26,9 +26,9 @@
 ORDER = (
     "aS0", "aT0", "aS1", "T1", "aG0", "aS2", "F0", "G0", "aT1", "oA0", "oD0", "oG0", "F1", "aT2", "aG1", "G1",
     "aG2", "F2", "G2", "nA0", "nD0", "nG0", "rS0", "oA1", "oD1", "oG1", "nA1", "nD1", "rM0", "nG1", "rS1",
-    "oA2", "oD2", "oG2", "rT0", "rM1", "nA2", "nD2", "nG2", "rS2", "rX0", "rT1", "rM2", "rFirst0", "bS0",
+    "oA2", "oD2", "oG2", "rT0", "rM1", "nA2", "nD2", "nG2", "rS2", "rT1", "rX0", "rM2", "rFirst0", "bS0",
     "rX1", "rT2", "bT0", "rFirst1", "bS1", "rX2", "bG0", "rFirst2", "N0", "bS2", "N1", "bT1", "N2", "pA0",
-    "N3", "bT2", "pD0", "pG0", "bG1", "qS0", "bG2", "pA1", "qM0", "pD1", "pG1", "qS1", "pA2", "qT0", "pD2",
+    "N3", "bT2", "bG1", "pD0", "pG0", "qS0", "bG2", "pA1", "qM0", "pD1", "pG1", "qS1", "pA2", "qT0", "pD2",
     "pG2", "qS2", "qM1", "qP0", "qM2", "qC0", "qT1", "qT2", "qP1", "qP2", "qC1", "qC2",
 )
 

time: 142 us -> 142 us (level)
  no operation moved by 1% of the time
where the time goes in v6:
time: 142 us
  Pallas kernels  139 us (98%)
  other arithmetic  2.18 us (2%)
    pallas_call x1, Pallas kernels, body(): pl.pallas_call(kernel, out_shape=jax.ShapeDtypeStruct((ROWS, DO), BF16),...  139 us

profile of v6, /device:TPU:1, one launch (start us, length us, event | category | flops | bytes accessed | tf_op | source)
XLA Modules:
  0.0 141.5 jit_solution(6181664425907114601)
XLA Ops:
  0.0 139.3 %shard_map.37 = bf16[96,3072]{1,0:T(8,128)(2,1)} custom-call(bf16[384,3072]{1,0:T(8,128)(2,1)} %feat.1, bf16[384,3072]{1,0:T(8,128)(2,1)} %cot.1, bf16[96,3072]{1,0:T(8,128)(2,1)} %weight.1), custom_call_target="tpu_custom_call" | custom-call | tf_op jit(solution)/shard_map/pallas_call | solution.py:446
  139.3 2.2 %convert_element_type.3 = f32[96,3072]{1,0:T(8,128)} convert(bf16[96,3072]{1,0:T(8,128)(2,1)} %shard_map.37) | non-fusion elementwise | flops 294912 | bytes 1769472 | tf_op jit(solution)/shard_map/convert_element_type | solution.py:477

commit v7 on v6

--- a/solution.py
+++ b/solution.py
@@ -25,8 +25,8 @@
 CUBIC = 0.044715
 ORDER = (
     "aS0", "aT0", "aS1", "T1", "aG0", "aS2", "F0", "G0", "aT1", "oA0", "oD0", "oG0", "F1", "aT2", "aG1", "G1",
-    "aG2", "F2", "G2", "nA0", "nD0", "nG0", "rS0", "oA1", "oD1", "oG1", "nA1", "nD1", "rM0", "nG1", "rS1",
-    "oA2", "oD2", "oG2", "rT0", "rM1", "nA2", "nD2", "nG2", "rS2", "rT1", "rX0", "rM2", "rFirst0", "bS0",
+    "aG2", "F2", "G2", "nA0", "nD0", "nG0", "rS0", "oA1", "oD1", "oG1", "rM0", "nA1", "nD1", "nG1", "rS1",
+    "oA2", "oD2", "oG2", "rT0", "rM1", "nA2", "nD2", "nG2", "rS2", "rX0", "rT1", "rM2", "rFirst0", "bS0",
     "rX1", "rT2", "bT0", "rFirst1", "bS1", "rX2", "bG0", "rFirst2", "N0", "bS2", "N1", "bT1", "N2", "pA0",
     "N3", "bT2", "bG1", "pD0", "pG0", "qS0", "bG2", "pA1", "qM0", "pD1", "pG1", "qS1", "pA2", "qT0", "pD2",
     "pG2", "qS2", "qM1", "qP0", "qM2", "qC0", "qT1", "qT2", "qP1", "qP2", "qC1", "qC2",

time: 142 us -> 142 us (level)
  no operation moved by 1% of the time
where the time goes in v7:
time: 142 us
  Pallas kernels  140 us (99%)
  other arithmetic  2.18 us (2%)
    pallas_call x1, Pallas kernels, body(): pl.pallas_call(kernel, out_shape=jax.ShapeDtypeStruct((ROWS, DO), BF16),...  140 us

profile of v7, /device:TPU:1, one launch (start us, length us, event | category | flops | bytes accessed | tf_op | source)
XLA Modules:
  0.0 141.9 jit_solution(9957005083892522077)
XLA Ops:
  0.0 139.7 %shard_map.37 = bf16[96,3072]{1,0:T(8,128)(2,1)} custom-call(bf16[384,3072]{1,0:T(8,128)(2,1)} %feat.1, bf16[384,3072]{1,0:T(8,128)(2,1)} %cot.1, bf16[96,3072]{1,0:T(8,128)(2,1)} %weight.1), custom_call_target="tpu_custom_call" | custom-call | tf_op jit(solution)/shard_map/pallas_call | solution.py:446
  139.7 2.2 %convert_element_type.3 = f32[96,3072]{1,0:T(8,128)} convert(bf16[96,3072]{1,0:T(8,128)(2,1)} %shard_map.37) | non-fusion elementwise | flops 294912 | bytes 1769472 | tf_op jit(solution)/shard_map/convert_element_type | solution.py:477
